TPU v7x, 32 devices: a whole 2x2x4 slice. The times are simulated.
32 devices in a mesh: dp: 16 (over z, y, core), seq: 2 (over x).
Axes of the slice: x: 2, y: 2, z: 4, core: 2. Of those that a mesh axis runs over, the one named last changes fastest.
Arguments:
- tile_feats: bfloat16 [8192, 2048], P('dp'), may hold values from -6 to 6
- tile_pos: int32 [16, 512], P('dp'), may hold values from -1 to 511, as said below
- slide_count: int32 [16], P('dp'), may hold values from 128 to 512, as said below
- w_proj: bfloat16 [2048, 768], P(None, 'seq'), may hold values from -0.125 to 0.125
- emb_grad: bfloat16 [16, 512, 768], P('dp', 'seq'), may hold values from -6 to 6
- ln_gain: float32 [768], replicated, may hold values from 0.25 to 1.75
- w_qkv: bfloat16 [768, 2304], P('dp'), may hold values from -1.5 to 1.5
- w_out: bfloat16 [768, 768], P('dp'), may hold values from -0.21875 to 0.21875
Outputs:
- slide_emb: bfloat16 [16, 512, 768], P('dp', 'seq')
- attn_branch: bfloat16 [16, 512, 768], P('dp', 'seq')
- proj_grad: float32 [2048, 768], P(None, 'seq')
Inputs may be any that keep to these rules, and one draw needn't show every extreme that they name: `tile_pos`: slot j of a row belongs to slide j // 32. Each position below a slide's slide_count is held by exactly one slot of that slide over all rows; all other slots hold -1. `slide_count`: some slide is full.
All inputs are finite; a program needn't handle non-finite values.
Results may differ from a plain program's by a relative error of at most 0.017.
The roundings to bfloat16 on the way count: a program that leaves them out, or rounds other values in their place, can miss the bound.
Values may be sent and summed in bfloat16 or wider, within the bound.
A program may use at most 128 MiB of HBM per device.

v0:
```python
import jax
import jax.numpy as jnp
from jax import lax
from jax.sharding import PartitionSpec as P

D = 768
HEAD_COUNT = 12
HEAD_WIDTH = 64
DILATION_STEP = 4


NEGATIVE = -1e30
EPSILON = 1e-05


def selection_shift(values, heads, dilation):
    length = values.shape[1]
    rest = values.shape[2:]
    shaped = values.reshape((heads, length // dilation, dilation) + rest)
    return jnp.stack(
        [shaped[head_number, :, head_number % dilation] for head_number in range(heads)]
    )


def insertion_shift(values, chosen, heads, dilation):
    length = values.shape[1]
    rest = values.shape[2:]
    shaped = values.reshape((heads, length // dilation, dilation) + rest)
    shift_amounts = jnp.arange(heads, dtype=jnp.int32) % dilation
    select = jnp.arange(dilation, dtype=jnp.int32)[None, :] == shift_amounts[:, None]
    select = select.reshape((heads, 1, dilation) + (1,) * len(rest))
    merged = jnp.where(select, chosen[:, :, None], shaped)
    return merged.reshape(values.shape)


def local(tile_feats, tile_pos, slide_count, w_proj, emb_grad, ln_gain, w_qkv, w_out):
    seq_count = lax.axis_size("seq")
    seq_index = lax.axis_index("seq")
    slot_rows = tile_feats.shape[0]
    nearby_length = emb_grad.shape[1]
    slide_len = nearby_length * seq_count
    inner = HEAD_COUNT * HEAD_WIDTH
    scale = HEAD_WIDTH ** (-0.5)
    tile_count = slide_count[0]
    emb_part = jnp.dot(tile_feats, w_proj, preferred_element_type=jnp.float32).astype(jnp.bfloat16)
    feature_part = emb_part.shape[1]
    positions = tile_pos.reshape(slot_rows)
    arrived, arrived_pos = (
        lax.all_to_all(emb_part, "dp", split_axis=0, concat_axis=0, tiled=True),
        lax.all_to_all(positions, "dp", split_axis=0, concat_axis=0, tiled=True),
    )
    target = jnp.where(arrived_pos >= 0, arrived_pos, slide_len).astype(jnp.int32)
    slide_rows = (
        jnp.zeros((slide_len + 1, feature_part), jnp.bfloat16).at[target].set(arrived)[:slide_len]
    )
    local_emb = lax.all_to_all(slide_rows, "seq", split_axis=0, concat_axis=1, tiled=True)
    widened = local_emb.astype(jnp.float32)
    center = jnp.mean(widened, axis=-1, keepdims=True)
    spread = jnp.mean(jnp.square(widened - center), axis=-1, keepdims=True)
    normed = ((widened - center) * lax.rsqrt(spread + EPSILON) * ln_gain).astype(jnp.bfloat16)
    columns = normed
    projected = jnp.dot(
        columns, lax.all_gather(w_qkv, "dp", axis=0, tiled=True), preferred_element_type=jnp.float32
    )
    projected = projected.astype(jnp.bfloat16)
    query_rows = projected[:, :inner].reshape(nearby_length, HEAD_COUNT, HEAD_WIDTH)
    key_matrix = projected[:, inner : 2 * inner].reshape(nearby_length, HEAD_COUNT, HEAD_WIDTH)
    value_matrix = projected[:, 2 * inner :].reshape(nearby_length, HEAD_COUNT, HEAD_WIDTH)
    sequence_position = seq_index * nearby_length + jnp.arange(nearby_length, dtype=jnp.int32)
    occupied = sequence_position < tile_count
    shift_amounts = jnp.arange(HEAD_COUNT, dtype=jnp.int32) % DILATION_STEP
    local_scores = (
        jnp.einsum("qhd,khd->hqk", query_rows, key_matrix, preferred_element_type=jnp.float32)
        * scale
    )
    local_ok = jnp.broadcast_to(occupied[None, None, :], local_scores.shape)
    nearby_maximum = jnp.max(jnp.where(local_ok, local_scores, NEGATIVE), axis=-1)
    local_weight = jnp.where(local_ok, jnp.exp(local_scores - nearby_maximum[..., None]), 0.0)
    nearby_sum = jnp.sum(local_weight, axis=-1)
    nearby_accumulator = jnp.einsum("hqk,khd->hqd", local_weight, value_matrix.astype(jnp.float32))
    stepped_queries = query_rows.reshape(
        nearby_length // DILATION_STEP, DILATION_STEP, HEAD_COUNT, HEAD_WIDTH
    )
    selected_query = jnp.stack(
        [
            stepped_queries[:, head_number % DILATION_STEP, head_number, :]
            for head_number in range(HEAD_COUNT)
        ]
    )
    key_value = jnp.concatenate([key_matrix, value_matrix], axis=-1)
    flat_rows = key_value.reshape(nearby_length, HEAD_COUNT * 2 * HEAD_WIDTH)
    portion = lax.all_gather(flat_rows, "seq", axis=0, tiled=True)
    row_counts = portion.shape[0]
    head_split = (row_counts + DILATION_STEP - 1) // DILATION_STEP
    shaped = portion.reshape(row_counts, HEAD_COUNT, 2 * HEAD_WIDTH)
    leading_index = shift_amounts % DILATION_STEP
    index_of_row = (
        leading_index[:, None] + DILATION_STEP * jnp.arange(head_split, dtype=jnp.int32)[None, :]
    )
    inside = index_of_row < row_counts
    safe_index = jnp.minimum(index_of_row, row_counts - 1)
    head_index = jnp.arange(HEAD_COUNT, dtype=jnp.int32)[:, None]
    chosen = shaped[safe_index, head_index, :]
    key_ok = inside & (index_of_row < tile_count)
    previous_maximum = selection_shift(nearby_maximum, HEAD_COUNT, DILATION_STEP)
    previous_sum = selection_shift(nearby_sum, HEAD_COUNT, DILATION_STEP)
    previous_accumulator = selection_shift(nearby_accumulator, HEAD_COUNT, DILATION_STEP)
    far_scores = (
        jnp.einsum(
            "hqd,hkd->hqk",
            selected_query,
            chosen[..., :HEAD_WIDTH],
            preferred_element_type=jnp.float32,
        )
        * scale
    )
    usable = jnp.broadcast_to(key_ok[:, None, :], far_scores.shape)
    new_max = jnp.maximum(
        previous_maximum, jnp.max(jnp.where(usable, far_scores, NEGATIVE), axis=-1)
    )
    far_weight = jnp.where(usable, jnp.exp(far_scores - new_max[..., None]), 0.0)
    rescale = jnp.exp(previous_maximum - new_max)
    updated_sum = previous_sum * rescale + jnp.sum(far_weight, axis=-1)
    updated_accumulator = previous_accumulator * rescale[..., None] + jnp.einsum(
        "hqk,hkd->hqd", far_weight, chosen[..., HEAD_WIDTH:].astype(jnp.float32)
    )
    complete_sum = insertion_shift(nearby_sum, updated_sum, HEAD_COUNT, DILATION_STEP)
    complete_accumulator = insertion_shift(
        nearby_accumulator, updated_accumulator, HEAD_COUNT, DILATION_STEP
    )
    safe_total = jnp.where(occupied[None, :], complete_sum, 1.0)
    context = jnp.where(occupied[None, :, None], complete_accumulator / safe_total[..., None], 0.0)
    context = context.transpose(1, 0, 2).reshape(nearby_length, inner).astype(jnp.bfloat16)
    columns = context
    branch_out = jnp.dot(
        columns, lax.all_gather(w_out, "dp", axis=0, tiled=True), preferred_element_type=jnp.float32
    )
    attn_branch = branch_out.astype(jnp.bfloat16)
    returned_grad = lax.all_to_all(
        emb_grad.reshape(nearby_length, D), "seq", split_axis=1, concat_axis=0, tiled=True
    )
    padded_grad = jnp.concatenate(
        [returned_grad, jnp.zeros((1, feature_part), jnp.bfloat16)], axis=0
    )
    picked_grad = padded_grad[target]
    slot_grad = lax.all_to_all(picked_grad, "dp", split_axis=0, concat_axis=0, tiled=True)
    grad_part = lax.dot_general(
        tile_feats, slot_grad, (((0,), (0,)), ((), ())), preferred_element_type=jnp.float32
    )
    proj_grad = lax.psum(grad_part, "dp")
    return (local_emb[None], attn_branch[None], proj_grad)


def solution(mesh):
    in_specs = (
        P("dp", None),
        P("dp", None),
        P("dp"),
        P(None, "seq"),
        P("dp", "seq", None),
        P(),
        P("dp", None),
        P("dp", None),
    )
    out_specs = (P("dp", "seq", None), P("dp", "seq", None), P(None, "seq"))
    return jax.shard_map(local, mesh=mesh, in_specs=in_specs, out_specs=out_specs, check_vma=False)
```

profile of v0, /device:TPU:0, one launch (start us, length us, event | category | flops | bytes accessed | tf_op | source)
XLA Modules:
  0.0 267.3 jit_solution(15064173347911541342)
XLA Ops:
  8.4 1.3 reduce.56
  10.5 7.4 %all-to-all-start = ((s32[16,32,1]{1,2,0:T(1,128)}), s32[16,32,1]{1,2,0:T(1,128)S(1)}, u32[]{:S(2)}, u32[]{:S(2)}) async-start(s32[16,32,1]{1,2,0:T(1,128)} %all_to_all.50), calls=%async_computation | async-start | bytes 16384 | tf_op jit(solution)/shard_map/all_to_all | solution.py:50
  17.9 3.5 %convolution_convert_fusion.2 = bf16[512,384]{1,0:T(8,128)(2,1)} fusion(bf16[512,2048]{1,0:T(8,128)(2,1)S(1)} %copy-done, bf16[2048,384]{1,0:T(8,128)(2,1)} %param.11), kind=kOutput, calls=%fused_computation.14 | convolution fusion | flops 805502976 | bytes 4063232 | tf_op jit(solution)/shard_map/dot_general | solution.py:45
  21.3 2.9 %all-to-all-done = s32[16,32,1]{1,2,0:T(1,128)S(1)} async-done(((s32[16,32,1]{1,2,0:T(1,128)}), s32[16,32,1]{1,2,0:T(1,128)S(1)}, u32[]{:S(2)}, u32[]{:S(2)}) %all-to-all-start) | async-done | bytes 2080 | tf_op jit(solution)/shard_map/all_to_all | solution.py:50
  24.2 3.6 %all-to-all-start.1 = ((bf16[16,32,384]{2,1,0:T(8,128)(2,1)}), bf16[16,32,384]{2,1,0:T(8,128)(2,1)S(1)}, u32[]{:S(2)}, u32[]{:S(2)}) async-start(bf16[16,32,384]{2,1,0:T(8,128)(2,1)} %bitcast.1), calls=%async_computation.1 | async-start | bytes 786432 | tf_op jit(solution)/shard_map/all_to_all | solution.py:49
  29.4 12.1 %all-to-all-done.1 = bf16[16,32,384]{2,1,0:T(8,128)(2,1)S(1)} async-done(((bf16[16,32,384]{2,1,0:T(8,128)(2,1)}), bf16[16,32,384]{2,1,0:T(8,128)(2,1)S(1)}, u32[]{:S(2)}, u32[]{:S(2)}) %all-to-all-start.1) | async-done | bytes 393248 | tf_op jit(solution)/shard_map/all_to_all | solution.py:49
  42.2 3.5 %all-to-all-start.3 = ((bf16[256,2,384]{2,0,1:T(8,128)(2,1)}), bf16[256,2,384]{2,0,1:T(8,128)(2,1)S(1)}, u32[]{:S(2)}, u32[]{:S(2)}) async-start(bf16[256,2,384]{2,0,1:T(8,128)(2,1)} %copy.164), calls=%async_computation.3 | async-start | bytes 786432 | tf_op jit(solution)/shard_map/all_to_all | solution.py:139
  45.7 2.9 %scatter_custom_fusion = bf16[513,384]{1,0:T(8,128)(2,1)S(1)} fusion(s32[512]{0:T(512)S(1)} %bitcast.199, bf16[512,384]{1,0:T(8,128)(2,1)} %bitcast.185, bf16[]{:T(256)} %constant.24.clone.1), kind=kCustom, calls=%fused_computation.31 | custom fusion | bytes 394496 | tf_op jit(solution)/shard_map/scatter | solution.py:54
  49.4 3.2 %all-to-all-done.3 = bf16[256,2,384]{2,0,1:T(8,128)(2,1)S(1)} async-done(((bf16[256,2,384]{2,0,1:T(8,128)(2,1)}), bf16[256,2,384]{2,0,1:T(8,128)(2,1)S(1)}, u32[]{:S(2)}, u32[]{:S(2)}) %all-to-all-start.3) | async-done | bytes 393248 | tf_op jit(solution)/shard_map/all_to_all | solution.py:139
  52.6 3.5 %all-to-all-start.2 = ((bf16[2,256,384]{2,1,0:T(8,128)(2,1)}), bf16[2,256,384]{2,1,0:T(8,128)(2,1)S(1)}, u32[]{:S(2)}, u32[]{:S(2)}) async-start(bf16[2,256,384]{2,1,0:T(8,128)(2,1)} %bitcast.3), calls=%async_computation.2 | async-start | bytes 786432 | tf_op jit(solution)/shard_map/all_to_all | solution.py:56
  56.1 2.6 gather_fusion.1
  58.7 3.5 %all-to-all-done.2 = bf16[2,256,384]{2,1,0:T(8,128)(2,1)S(1)} async-done(((bf16[2,256,384]{2,1,0:T(8,128)(2,1)}), bf16[2,256,384]{2,1,0:T(8,128)(2,1)S(1)}, u32[]{:S(2)}, u32[]{:S(2)}) %all-to-all-start.2) | async-done | bytes 393248 | tf_op jit(solution)/shard_map/all_to_all | solution.py:56
  62.1 4.8 %all-to-all-start.4 = ((bf16[16,32,384]{2,1,0:T(8,128)(2,1)}), bf16[16,32,384]{2,1,0:T(8,128)(2,1)}, u32[]{:S(2)}, u32[]{:S(2)}) async-start(bf16[16,32,384]{2,1,0:T(8,128)(2,1)} %bitcast.50), calls=%async_computation.4 | async-start | bytes 786432 | tf_op jit(solution)/shard_map/all_to_all | solution.py:146
  67.9 1.4 copy.125
  69.3 9.9 %all-to-all-done.4 = bf16[16,32,384]{2,1,0:T(8,128)(2,1)} async-done(((bf16[16,32,384]{2,1,0:T(8,128)(2,1)}), bf16[16,32,384]{2,1,0:T(8,128)(2,1)}, u32[]{:S(2)}, u32[]{:S(2)}) %all-to-all-start.4) | async-done | bytes 393248 | tf_op jit(solution)/shard_map/all_to_all | solution.py:146
  79.2 3.7 %convolution_bitcast_fusion = f32[2048,384]{0,1:T(8,128)} fusion(bf16[512,384]{1,0:T(8,128)(2,1)} %bitcast.51, bf16[512,2048]{1,0:T(8,128)(2,1)S(1)} %copy-done), kind=kOutput, calls=%fused_computation.6 | convolution fusion | flops 805306368 | bytes 5636096 | tf_op jit(solution)/shard_map/dot_general | solution.py:147
  84.4 3.5 %convolution_convert_fusion = bf16[256,2304]{1,0:T(8,128)(2,1)S(1)} fusion(bf16[256,768]{0,1:T(8,128)(2,1)} %fusion.9, bf16[768,2304]{1,0:T(8,128)(2,1)} %all-gather.4.cloned.1.call-done), kind=kOutput, calls=%fused_computation.3 | convolution fusion | flops 906559488 | bytes 5111808 | tf_op jit(solution)/shard_map/dot_general | solution.py:62
  89.7 1.2 copy.127
  90.8 2.0 pad_maximum_fusion
  95.3 1.9 copy.165
  97.2 87.1 %all-reduce.3.cloned.1.call-done = f32[2048,384]{0,1:T(8,128)} async-done(((f32[2048,384]{0,1:T(8,128)}), f32[2048,384]{0,1:T(8,128)}) %all-reduce.3.cloned.1.call-update) | async-done | bytes 3145744 | tf_op jit(solution)/shard_map/psum | solution.py:150
  184.4 3.5 %copy.166 = f32[2048,384]{1,0:T(8,128)} copy(f32[2048,384]{0,1:T(8,128)} %all-reduce.3.cloned.1.call-done) | data formatting | bytes 6291456
  188.1 1.6 reshape_reshape.3
  189.7 2.4 select_reduce_fusion
  192.1 2.8 %fusion.1 = f32[12,256,64]{1,2,0:T(8,128)S(1)} fusion(bf16[256,12,64]{0,2,1:T(8,128)(2,1)} %bitcast.181, f32[12,256,256]{1,2,0:T(8,128)} %get-tuple-element.69, f32[12,256]{1,0:T(8,128)S(1)} %get-tuple-element.68, pred[256]{0:T(512)(128)(4,1)S(1)} %add_compare_fusion.2), kind=kOutput, calls=%fused_computation.8 | convolution fusion | flops 103022592 | bytes 4337920 | tf_op jit(solution)/shard_map/hqk,khd->hqd/dot_general | solution.py:80
  195.9 1.7 copy.130
  197.6 2.5 fusion.27
  200.7 2.6 fusion.29
  203.3 3.4 %slice_reduce_fusion.12 = (f32[64]{0:T(128)S(1)}, f32[64]{0:T(128)S(1)}, f32[64]{0:T(128)S(1)}, f32[64]{0:T(128)}, f32[64]{0:T(128)}, /*index=5*/f32[64]{0:T(128...) fusion(f32[12,64,4]{0,2,1:T(4,128)S(1)} %bitcast.175), kind=kLoop, calls=%fused_computation.72 | loop fusion | bytes 6144 | tf_op jit(solution)/shard_map/slice | solution.py:21
  206.8 3.4 %slice_reduce_fusion = (f32[64]{0:T(128)}, f32[64]{0:T(128)}, f32[64]{0:T(128)}, f32[64]{0:T(128)}, f32[64]{0:T(128)}, /*index=5*/f32[64]{0:T(128)}, f32[64]{0:T...) fusion(f32[12,64,4]{0,2,1:T(4,128)S(1)} %bitcast.176), kind=kLoop, calls=%fused_computation.60 | loop fusion | bytes 6144 | tf_op jit(solution)/shard_map/slice | solution.py:21
  210.1 1.4 constant_dynamic-update-slice_fusion.10
  211.5 1.4 constant_dynamic-update-slice_fusion.9
  212.9 1.4 constant_dynamic-update-slice_fusion.8
  214.3 1.4 constant_dynamic-update-slice_fusion.7
  215.6 1.4 constant_dynamic-update-slice_fusion.6
  217.0 1.4 constant_dynamic-update-slice_fusion.5
  218.4 1.4 constant_dynamic-update-slice_fusion.4
  219.8 1.4 constant_dynamic-update-slice_fusion.3
  221.1 1.4 constant_dynamic-update-slice_fusion.2
  226.2 1.3 stack.73
  227.6 1.4 stack.87
  229.7 2.6 copy.156
  232.3 17.9 %gather_fusion = bf16[1536,128]{1,0:T(8,128)(2,1)S(1)} fusion(bf16[512,12,128]{2,0,1:T(8,128)(2,1)} %copy.156, s32[1536]{0:T(1024)S(1)} %fusion.21), kind=kCustom, calls=%fused_computation | custom fusion | bytes 798720 | tf_op jit(solution)/shard_map/gather | solution.py:103
  251.0 1.4 convolution_add_fusion
  252.5 1.5 broadcast_in_dim.146
  253.9 2.8 %copy.159 = f32[12,256,64]{1,2,0:T(8,128)} copy(f32[12,256,64]{2,1,0:T(8,128)} %bitcast.168) | data formatting | bytes 1572864 | tf_op jit(solution)/shard_map/jit(_where)/broadcast_in_dim | solution.py:32
  256.9 1.4 select_convert_fusion
  258.3 2.5 fusion.6
  (76 shorter events, 18.7 us)
Async XLA Ops:
  7.2 10.7 %copy-start = (bf16[512,2048]{1,0:T(8,128)(2,1)S(1)}, bf16[512,2048]{1,0:T(8,128)(2,1)}, u32[]{:S(2)}) copy-start(bf16[512,2048]{1,0:T(8,128)(2,1)} %param.8) | copy-start | bytes 6291460
  7.2 77.3 %all-gather.4.cloned.1.call-start = ((), (), s32[]{:S(2)}) async-start(), calls=%async_computation.5 | async-start | bytes 3760128 | tf_op jit(solution)/shard_map/all_gather | solution.py:63
  10.5 13.7 %all-to-all-start = ((s32[16,32,1]{1,2,0:T(1,128)}), s32[16,32,1]{1,2,0:T(1,128)S(1)}, u32[]{:S(2)}, u32[]{:S(2)}) async-start(s32[16,32,1]{1,2,0:T(1,128)} %all_to_all.50), calls=%async_computation | async-start | bytes 16384 | tf_op jit(solution)/shard_map/all_to_all | solution.py:50
  17.9 9.9 %copy-start.2 = (bf16[1,256,768]{2,1,0:T(8,128)(2,1)S(1)}, bf16[1,256,768]{2,1,0:T(8,128)(2,1)}, u32[]{:S(2)}) copy-start(bf16[1,256,768]{2,1,0:T(8,128)(2,1)} %param.12) | copy-start | bytes 1179652
  24.2 17.3 %all-to-all-start.1 = ((bf16[16,32,384]{2,1,0:T(8,128)(2,1)}), bf16[16,32,384]{2,1,0:T(8,128)(2,1)S(1)}, u32[]{:S(2)}, u32[]{:S(2)}) async-start(bf16[16,32,384]{2,1,0:T(8,128)(2,1)} %bitcast.1), calls=%async_computation.1 | async-start | bytes 786432 | tf_op jit(solution)/shard_map/all_to_all | solution.py:49
  41.5 0.7 copy-start.3
  42.2 10.3 %all-to-all-start.3 = ((bf16[256,2,384]{2,0,1:T(8,128)(2,1)}), bf16[256,2,384]{2,0,1:T(8,128)(2,1)S(1)}, u32[]{:S(2)}, u32[]{:S(2)}) async-start(bf16[256,2,384]{2,0,1:T(8,128)(2,1)} %copy.164), calls=%async_computation.3 | async-start | bytes 786432 | tf_op jit(solution)/shard_map/all_to_all | solution.py:139
  52.6 9.6 %all-to-all-start.2 = ((bf16[2,256,384]{2,1,0:T(8,128)(2,1)}), bf16[2,256,384]{2,1,0:T(8,128)(2,1)S(1)}, u32[]{:S(2)}, u32[]{:S(2)}) async-start(bf16[2,256,384]{2,1,0:T(8,128)(2,1)} %bitcast.3), calls=%async_computation.2 | async-start | bytes 786432 | tf_op jit(solution)/shard_map/all_to_all | solution.py:56
  62.1 17.0 %all-to-all-start.4 = ((bf16[16,32,384]{2,1,0:T(8,128)(2,1)}), bf16[16,32,384]{2,1,0:T(8,128)(2,1)}, u32[]{:S(2)}, u32[]{:S(2)}) async-start(bf16[16,32,384]{2,1,0:T(8,128)(2,1)} %bitcast.50), calls=%async_computation.4 | async-start | bytes 786432 | tf_op jit(solution)/shard_map/all_to_all | solution.py:146
  66.9 117.5 %all-reduce.3.cloned.1.call-start = ((), (), s32[]{:S(2)}) async-start(), calls=%async_computation.8 | async-start | bytes 6291456 | tf_op jit(solution)/shard_map/psum | solution.py:150
  82.8 0.7 copy-start.4
  82.9 146.8 %all-gather.6.cloned.1.call-start = ((), (), s32[]{:S(2)}) async-start(), calls=%async_computation.6 | async-start | bytes 2359296 | tf_op jit(solution)/shard_map/all_gather | solution.py:92
  92.8 165.5 %all-gather.8.cloned.1.call-start = ((), (), s32[]{:S(2)}) async-start(), calls=%async_computation.7 | async-start | bytes 1253376 | tf_op jit(solution)/shard_map/all_gather | solution.py:136
  192.1 3.1 %copy-start.1 = (f32[12,256,256]{1,2,0:T(8,128)S(1)}, f32[12,256,256]{1,2,0:T(8,128)}, u32[]{:S(2)}) copy-start(f32[12,256,256]{1,2,0:T(8,128)} %get-tuple-element.69) | copy-start | bytes 9437188
Sparse Core Ops, SparseCore 0:
  10.3 52.3 all-gather.3
  83.0 101.3 all-reduce.2
  185.9 26.3 all-gather.5
  214.4 38.3 all-gather.7
where the time goes:
time: 269 us; the launch traced here: 267 us
  waiting for transfers between devices  120 us (45%)
  local copies, waits for them, and re-layouts  81 us (30%)
  starting transfers between devices  23 us (9%)
  matrix products  20.2 us (8%)
  between operations  14.7 us (5%)
  other arithmetic  8.78 us (3%)
    psum x1, waiting for transfers between devices, local(): proj_grad = lax.psum(grad_part, 'dp')  87.1 us
    unnamed x35, local copies, waits for them, and re-layouts  24 us
    gather x1, local copies, waits for them, and re-layouts, local(): chosen = shaped[safe_index, head_index, :]  17.9 us
    all_to_all x1, waiting for transfers between devices, local(): lax.all_to_all(emb_part, 'dp', split_axis=0, concat_axis=0, tiled=True)  12.1 us
    all_to_all x1, waiting for transfers between devices, local(): lax.all_to_all(picked_grad, 'dp', split_axis=0, concat_axis=0, tiled=True)  9.87 us
    slice x3, local copies, waits for them, and re-layouts, selection_shift(): shaped[head_number, :, head_number % dilation]  9.23 us
    all_to_all x1, starting transfers between devices, local(): lax.all_to_all(positions, 'dp', split_axis=0, concat_axis=0, tiled=True)  7.39 us
  transfers between devices with their start and end apart: 9, of which 6 were waited for; matrix products, arithmetic and copies ran while one was open for 39% of the time, Pallas kernels for 0%

commit v1 on v0

v1 whole, which is shorter than its diff:
```python
import functools

import jax
import jax.numpy as jnp
from jax import lax
from jax.experimental import pallas as pl
from jax.experimental.pallas import tpu as pltpu
from jax.sharding import PartitionSpec as P

D = 768
HEAD_COUNT = 12
HEAD_WIDTH = 64
DILATION_STEP = 4
NEGATIVE = -1e30
EPSILON = 1e-05
STEP_HEADS = 4

F32 = jnp.float32
BF16 = jnp.bfloat16


def put_rows(whole, rows, low, high):
    pieces = [whole[:low]] if low else []
    pieces.append(rows)
    if high < whole.shape[0]:
        pieces.append(whole[high:])
    return jnp.concatenate(pieces, axis=0)


def attention_kernel(
    seq_count,
    nearby,
    meta_ref,
    rows_ref,
    gain_ref,
    wq_ref,
    wk_ref,
    wv_ref,
    wo_ref,
    emb_ref,
    branch_ref,
    normed,
    context,
):
    step = pl.program_id(0)
    me = meta_ref[0]
    count = meta_ref[1]
    part = nearby // DILATION_STEP
    own = pl.multiple_of(me * nearby, nearby)

    @pl.when(step == 0)
    def _():
        for block in range(seq_count):
            at = slice(block * nearby, (block + 1) * nearby)
            wide = jnp.concatenate(
                [rows_ref[c, at, :] for c in range(seq_count)], axis=-1
            ).astype(F32)
            center = jnp.mean(wide, axis=-1, keepdims=True)
            spread = jnp.mean(jnp.square(wide - center), axis=-1, keepdims=True)
            normed[at, :] = (
                (wide - center) * lax.rsqrt(spread + EPSILON) * gain_ref[...]
            ).astype(BF16)

    mine = normed[pl.ds(own, nearby), :]
    query = jnp.dot(mine, wq_ref[...], preferred_element_type=F32).astype(BF16)
    query = query * BF16(HEAD_WIDTH**-0.5)
    key = jnp.dot(mine, wk_ref[...], preferred_element_type=F32).astype(BF16)
    value = jnp.dot(mine, wv_ref[...], preferred_element_type=F32).astype(BF16)
    far_keys, far_values = [], []
    for other in range(1, seq_count):
        block = lax.rem(me + other, seq_count)
        start = pl.multiple_of(block * nearby, nearby)
        theirs = normed[pl.ds(start, nearby), :]
        far_keys.append(jnp.dot(theirs, wk_ref[...], preferred_element_type=F32).astype(BF16))
        far_values.append(jnp.dot(theirs, wv_ref[...], preferred_element_type=F32).astype(BF16))

    lane = lax.broadcasted_iota(jnp.int32, (1, nearby), 1)
    key_ok = own + (lane % part) * DILATION_STEP + lane // part < count
    row = lax.broadcasted_iota(jnp.int32, (nearby, 1), 0)
    query_ok = own + (row % part) * DILATION_STEP + row // part < count
    far_lane = lax.broadcasted_iota(jnp.int32, (1, part * (seq_count - 1)), 1)
    far_block = lax.rem(me + 1 + far_lane // part, seq_count)
    far_spot = far_block * nearby + far_lane % part * DILATION_STEP
    dims = (((1,), (1,)), ((), ()))
    outs = []
    for head in range(STEP_HEADS):
        shift = head % DILATION_STEP
        cols = slice(head * HEAD_WIDTH, (head + 1) * HEAD_WIDTH)
        low, high = shift * part, (shift + 1) * part
        q, k, v = query[:, cols], key[:, cols], value[:, cols]
        scores = lax.dot_general(q, k, dims, preferred_element_type=F32)
        scores = jnp.where(key_ok, scores, NEGATIVE)
        maximum = jnp.max(scores, axis=-1, keepdims=True)
        far_k = jnp.concatenate([x[low:high, cols] for x in far_keys], axis=0)
        far_v = jnp.concatenate([x[low:high, cols] for x in far_values], axis=0)
        far_ok = far_spot + shift < count
        far = lax.dot_general(q[low:high], far_k, dims, preferred_element_type=F32)
        far = jnp.where(far_ok, far, NEGATIVE)
        far_max = jnp.maximum(maximum[low:high], jnp.max(far, axis=-1, keepdims=True))
        maximum = put_rows(maximum, far_max, low, high)
        weight = jnp.exp(scores - maximum)
        in_lane = (lane >= low) & (lane < high)
        twice = jnp.where(in_lane, weight[low:high] * 2.0, weight[low:high])
        weight = put_rows(weight, twice, low, high)
        far_weight = jnp.exp(far - far_max)
        total = jnp.sum(weight, axis=-1, keepdims=True)
        far_total = jnp.sum(far_weight, axis=-1, keepdims=True)
        total = put_rows(total, total[low:high] + far_total, low, high)
        gathered = jnp.dot(weight.astype(BF16), v, preferred_element_type=F32)
        far_gathered = jnp.dot(far_weight.astype(BF16), far_v, preferred_element_type=F32)
        gathered = put_rows(gathered, gathered[low:high] + far_gathered, low, high)
        outs.append(jnp.where(query_ok, gathered / total, 0.0).astype(BF16))
    context[step] = jnp.concatenate(outs, axis=-1)

    @pl.when(step == pl.num_programs(0) - 1)
    def _():
        at_row = lax.broadcasted_iota(jnp.int32, (nearby, nearby), 0)
        at_lane = lax.broadcasted_iota(jnp.int32, (nearby, nearby), 1)
        natural = (at_lane % part) * DILATION_STEP + at_lane // part
        back = jnp.where(at_row == natural, 1.0, 0.0).astype(BF16)
        ordered = jnp.concatenate(
            [rows_ref[c, pl.ds(own, nearby), :] for c in range(seq_count)], axis=-1
        )
        emb_ref[...] = jnp.dot(back, ordered, preferred_element_type=F32).astype(BF16)
        whole = jnp.concatenate(
            [context[i] for i in range(HEAD_COUNT // STEP_HEADS)], axis=-1
        )
        whole = jnp.dot(back, whole, preferred_element_type=F32).astype(BF16)
        branch_ref[...] = jnp.dot(whole, wo_ref[...], preferred_element_type=F32).astype(BF16)


def attend(meta, rows, gain, w_qkv, w_out, seq_count, nearby):
    width = STEP_HEADS * HEAD_WIDTH
    steps = HEAD_COUNT // STEP_HEADS
    slide_len = rows.shape[1]
    full = lambda *shape: pl.BlockSpec(shape, lambda i: (0,) * len(shape))
    out = jax.ShapeDtypeStruct((nearby, D), BF16)
    return pl.pallas_call(
        functools.partial(attention_kernel, seq_count, nearby),
        out_shape=(out, out),
        grid=(steps,),
        in_specs=[
            pl.BlockSpec(memory_space=pltpu.SMEM),
            full(*rows.shape),
            full(1, D),
            pl.BlockSpec((D, width), lambda i: (0, i)),
            pl.BlockSpec((D, width), lambda i: (0, steps + i)),
            pl.BlockSpec((D, width), lambda i: (0, 2 * steps + i)),
            full(D, D),
        ],
        out_specs=(full(nearby, D), full(nearby, D)),
        scratch_shapes=[
            pltpu.VMEM((slide_len, D), BF16),
            pltpu.VMEM((steps, nearby, width), BF16),
        ],
        compiler_params=pltpu.CompilerParams(vmem_limit_bytes=48 * 1024 * 1024),
        cost_estimate=pl.CostEstimate(
            flops=20_000_000_000, bytes_accessed=20_000_000, transcendentals=1_000_000
        ),
    )(meta, rows, gain, w_qkv, w_qkv, w_qkv, w_out)


def local(tile_feats, tile_pos, slide_count, w_proj, emb_grad, ln_gain, w_qkv, w_out):
    seq_count = lax.axis_size("seq")
    seq_index = lax.axis_index("seq")
    slot_rows = tile_feats.shape[0]
    nearby = emb_grad.shape[1]
    slide_len = nearby * seq_count
    part = nearby // DILATION_STEP
    positions = lax.all_to_all(
        tile_pos.reshape(slot_rows), "dp", split_axis=0, concat_axis=0, tiled=True
    )
    returned_grad = lax.all_to_all(
        emb_grad.reshape(nearby, D), "seq", split_axis=1, concat_axis=0, tiled=True
    )
    spot = jnp.arange(slide_len, dtype=jnp.int32)
    hot = (spot[:, None] == positions[None, :]).astype(BF16)
    picked_grad = lax.dot_general(
        hot, returned_grad, (((0,), (0,)), ((), ())), preferred_element_type=F32
    ).astype(BF16)
    slot_grad = lax.all_to_all(picked_grad, "dp", split_axis=0, concat_axis=0, tiled=True)
    grad_part = lax.dot_general(
        tile_feats, slot_grad, (((0,), (0,)), ((), ())), preferred_element_type=F32
    )
    proj_grad = lax.psum(grad_part.astype(BF16), "dp").astype(F32)

    emb_part = jnp.dot(tile_feats, w_proj, preferred_element_type=F32).astype(BF16)
    arrived = lax.all_to_all(emb_part, "dp", split_axis=0, concat_axis=0, tiled=True)
    inside = spot % nearby
    at_spot = spot - inside + (inside % part) * DILATION_STEP + inside // part
    hot_perm = (at_spot[:, None] == positions[None, :]).astype(BF16)
    slide_rows = jnp.dot(hot_perm, arrived, preferred_element_type=F32).astype(BF16)
    rows = lax.all_gather(slide_rows, "seq", axis=0, tiled=False)
    meta = jnp.stack([seq_index.astype(jnp.int32), slide_count[0]])
    local_emb, attn_branch = attend(
        meta,
        rows,
        ln_gain.reshape(1, D),
        lax.all_gather(w_qkv, "dp", axis=0, tiled=True),
        lax.all_gather(w_out, "dp", axis=0, tiled=True),
        seq_count,
        nearby,
    )
    return (local_emb[None], attn_branch[None], proj_grad)


def solution(mesh):
    in_specs = (
        P("dp", None),
        P("dp", None),
        P("dp"),
        P(None, "seq"),
        P("dp", "seq", None),
        P(),
        P("dp", None),
        P("dp", None),
    )
    out_specs = (P("dp", "seq", None), P("dp", "seq", None), P(None, "seq"))
    return jax.shard_map(local, mesh=mesh, in_specs=in_specs, out_specs=out_specs, check_vma=False)
```

time: 269 us -> 258 us (0.959)
  local copies, waits for them, and re-layouts: 81 us -> 9.76 us
  waiting for transfers between devices: 120 us -> 173 us
  blocking collectives: 0 us -> 26.3 us
  matrix products: 20.2 us -> 6.53 us
  Pallas kernels: 0 us -> 10.3 us
  starting transfers between devices: 23 us -> 14.5 us
  other arithmetic: 8.78 us -> 2.21 us
    all_gather x1, waiting for transfers between devices: 0.01 us -> 48.5 us  [local(): lax.all_gather(w_qkv, 'dp', axis=0, tiled=True)]
    all_gather x1, waiting for transfers between devices: 0.02 us -> 36.5 us  [local(): lax.all_gather(w_out, 'dp', axis=0, tiled=True)]
    psum x1, waiting for transfers between devices: 87.1 us -> 61.7 us  [local(): proj_grad = lax.psum(grad_part.astype(BF16), 'dp').astype(F32)]
    gather x2 -> x0, local copies, waits for them, and re-layouts: 20.5 us -> none  [the longest x1 17.9 us: local(): chosen = shaped[safe_index, head_index, :]]
    slice x9 -> x0, local copies, waits for them, and re-layouts: 15.7 us -> none  [the longest x3 9.23 us: selection_shift(): shaped[head_number, :, head_number % dilation]]
    unnamed x35 -> x11, local copies, waits for them, and re-layouts: 24 us -> 8.78 us
    all_to_all x0 -> x1, blocking collectives: none -> 14.8 us  [local(): lax.all_to_all(picked_grad, 'dp', split_axis=0, concat_axis=0, tiled=True)]
    dot_general x7 -> x3, matrix products: 16.5 us -> 4.38 us  [the longest x1 3.41 us: local(): jnp.dot(tile_feats, w_proj, preferred_element_type=F32).astype(BF16)]
  transfers between devices with their start and end apart: 9 -> 6, of which waited for: 6 -> 6; matrix products, arithmetic and copies ran while one was open for 39% -> 4% of each run, Pallas kernels for 0% -> 0%
where the time goes in v1:
time: 258 us; the launch traced here: 257 us
  waiting for transfers between devices  173 us (67%)
  blocking collectives  26.3 us (10%)
  starting transfers between devices  14.5 us (6%)
  between operations  14.5 us (6%)
  Pallas kernels  10.3 us (4%)
  local copies, waits for them, and re-layouts  9.76 us (4%)
  matrix products  6.53 us (3%)
    psum x1, waiting for transfers between devices, local(): proj_grad = lax.psum(grad_part.astype(BF16), 'dp').astype(F32)  61.7 us
    all_gather x1, waiting for transfers between devices, local(): lax.all_gather(w_qkv, 'dp', axis=0, tiled=True)  48.5 us
    all_gather x1, waiting for transfers between devices, local(): lax.all_gather(w_out, 'dp', axis=0, tiled=True)  36.5 us
    all_to_all x1, waiting for transfers between devices, local(): lax.all_to_all(emb_part, 'dp', split_axis=0, concat_axis=0, tiled=True)  14.9 us
    all_to_all x1, blocking collectives, local(): lax.all_to_all(picked_grad, 'dp', split_axis=0, concat_axis=0, tiled=True)  14.8 us
    all_gather x1, blocking collectives, local(): rows = lax.all_gather(slide_rows, 'seq', axis=0, tiled=False)  11.5 us
    pallas_call x1, Pallas kernels, attend(): pl.pallas_call(functools.partial(attention_kernel, seq_count, nearby), ou...  10.3 us
    unnamed x11, local copies, waits for them, and re-layouts  8.78 us
  transfers between devices with their start and end apart: 6, of which 6 were waited for; matrix products, arithmetic and copies ran while one was open for 4% of the time, Pallas kernels for 0%

profile of v1, /device:TPU:0, one launch (start us, length us, event | category | flops | bytes accessed | tf_op | source)
XLA Modules:
  0.0 257.4 jit_solution(2987965517971867592)
XLA Ops:
  7.2 0.0 copy-start
  7.2 0.5 broadcast.83
  7.7 1.5 reduce.6
  9.1 0.7 all_to_all.36
  9.8 7.4 %all-to-all-start = ((s32[16,32,1]{1,2,0:T(1,128)}), s32[16,32,1]{1,2,0:T(1,128)S(1)}, u32[]{:S(2)}, u32[]{:S(2)}) async-start(s32[16,32,1]{1,2,0:T(1,128)} %all_to_all.36), calls=%async_computation | async-start | bytes 16384 | tf_op jit(solution)/shard_map/all_to_all | solution.py:170
  17.2 1.9 copy.16
  19.1 4.4 %all-to-all-done = s32[16,32,1]{1,2,0:T(1,128)S(1)} async-done(((s32[16,32,1]{1,2,0:T(1,128)}), s32[16,32,1]{1,2,0:T(1,128)S(1)}, u32[]{:S(2)}, u32[]{:S(2)}) %all-to-all-start) | async-done | bytes 2080 | tf_op jit(solution)/shard_map/all_to_all | solution.py:170
  23.6 3.5 %all-to-all-start.2 = ((bf16[256,2,384]{0,2,1:T(8,128)(2,1)}), bf16[256,2,384]{0,2,1:T(8,128)(2,1)S(1)}, u32[]{:S(2)}, u32[]{:S(2)}) async-start(bf16[256,2,384]{0,2,1:T(8,128)(2,1)} %bitcast.6), calls=%async_computation.2 | async-start | bytes 786432 | tf_op jit(solution)/shard_map/all_to_all | solution.py:173
  27.0 0.0 all-reduce.2.cloned.1.call-start
  27.1 0.7 reduce.7
  27.8 0.1 eq.30
  27.8 6.0 %all-to-all-done.2 = bf16[256,2,384]{0,2,1:T(8,128)(2,1)S(1)} async-done(((bf16[256,2,384]{0,2,1:T(8,128)(2,1)}), bf16[256,2,384]{0,2,1:T(8,128)(2,1)S(1)}, u32[]{:S(2)}, u32[]{:S(2)}) %all-to-all-start.2) | async-done | bytes 393248 | tf_op jit(solution)/shard_map/all_to_all | solution.py:173
  33.8 0.2 copy.17
  34.0 0.5 convolution_convert_fusion.2
  34.5 14.8 %all_to_all.52 = bf16[16,32,384]{2,1,0:T(8,128)(2,1)S(1)} all-to-all(bf16[16,32,384]{2,1,0:T(8,128)(2,1)S(1)} %bitcast.25), channel_id=1, replica_groups=mesh['dp'=16,'seq'=2] {'dp'}, dimensions={0} | all-to-all | bytes 786432 | tf_op jit(solution)/shard_map/all_to_all | solution.py:181
  49.3 0.0 copy-done
  49.3 2.2 fusion
  51.5 0.0 all-reduce.2.cloned.1.call-update
  51.5 0.0 all-gather.6.cloned.1.call-start
  51.6 0.7 all-gather.6.cloned.1.call-update
  52.3 0.0 all-gather.4.cloned.1.call-start
  52.3 0.7 all-gather.4.cloned.1.call-update
  53.0 0.0 copy-start.3
  53.0 3.4 %convolution_convert_fusion.1 = bf16[512,384]{1,0:T(8,128)(2,1)} fusion(bf16[512,2048]{1,0:T(8,128)(2,1)S(1)} %copy-done, bf16[2048,384]{1,0:T(8,128)(2,1)} %param.11), kind=kOutput, calls=%fused_computation.2 | convolution fusion | flops 805502976 | bytes 4063232 | tf_op jit(solution)/shard_map/dot_general | solution.py:187
  56.4 3.6 %all-to-all-start.1 = ((bf16[16,32,384]{2,1,0:T(8,128)(2,1)}), bf16[16,32,384]{2,1,0:T(8,128)(2,1)S(1)}, u32[]{:S(2)}, u32[]{:S(2)}) async-start(bf16[16,32,384]{2,1,0:T(8,128)(2,1)} %bitcast.1), calls=%async_computation.1 | async-start | bytes 786432 | tf_op jit(solution)/shard_map/all_to_all | solution.py:188
  60.6 0.0 copy-done.3
  60.7 0.1 pad_add_fusion.meta_ref
  60.7 14.9 %all-to-all-done.1 = bf16[16,32,384]{2,1,0:T(8,128)(2,1)S(1)} async-done(((bf16[16,32,384]{2,1,0:T(8,128)(2,1)}), bf16[16,32,384]{2,1,0:T(8,128)(2,1)S(1)}, u32[]{:S(2)}, u32[]{:S(2)}) %all-to-all-start.1) | async-done | bytes 393248 | tf_op jit(solution)/shard_map/all_to_all | solution.py:188
  75.6 0.5 convolution_convert_fusion.3
  76.1 11.5 %all-gather = bf16[1024,384]{1,0:T(8,128)(2,1)S(1)} all-gather(bf16[512,384]{1,0:T(8,128)(2,1)S(1)} %convolution_convert_fusion.3), channel_id=2, replica_groups=mesh['dp'=16,'seq'=2] {'seq'}, dimensions={0}, use_global_device_ids=true | all-gather | bytes 1179648 | tf_op jit(solution)/shard_map/all_gather | solution.py:193
  87.6 61.7 %all-reduce.2.cloned.1.call-done = bf16[2048,384]{0,1:T(8,128)(2,1)} async-done(((bf16[2048,384]{0,1:T(8,128)(2,1)}), bf16[2048,384]{0,1:T(8,128)(2,1)}) %all-reduce.2.cloned.1.call-update) | async-done | bytes 1572880 | tf_op jit(solution)/shard_map/psum | solution.py:185
  149.3 3.1 %copy.18 = f32[2048,384]{1,0:T(8,128)} copy(bf16[2048,384]{0,1:T(8,128)(2,1)} %all-reduce.2.cloned.1.call-done) | data formatting | bytes 4718592
  152.4 36.5 %all-gather.6.cloned.1.call-done.wo_ref = bf16[768,768]{1,0:T(8,128)(2,1)} async-done(((bf16[48,768]{1,0:T(8,128)(2,1)}), bf16[768,768]{1,0:T(8,128)(2,1)}) %all-gather.6.cloned.1.call-update) | async-done | bytes 1179664 | tf_op jit(solution)/shard_map/all_gather | solution.py:200
  188.8 48.5 %all-gather.4.cloned.1.call-done.wq_ref.wk_ref.wv_ref = bf16[768,2304]{1,0:T(8,128)(2,1)} async-done(((bf16[48,2304]{1,0:T(8,128)(2,1)}), bf16[768,2304]{1,0:T(8,128)(2,1)}) %all-gather.4.cloned.1.call-update) | async-done | bytes 3538960 | tf_op jit(solution)/shard_map/all_gather | solution.py:199
  237.3 0.0 copy-start.1
  237.3 2.0 copy-done.1
  239.3 0.0 copy-start.2
  239.3 1.3 copy-done.2
  240.6 10.3 %shard_map.103 = (bf16[256,768]{1,0:T(8,128)(2,1)}, bf16[256,768]{1,0:T(8,128)(2,1)}) custom-call(s32[2]{0:T(128)S(1)} %pad_add_fusion.meta_ref, bf16[2,512,384]{2,1,0:T(8,128)(2,1)S(1)} %bitcast.20, f32[1,768]{1,0:T(1,128)S(1)} %reshape.64.gain_ref, bf16[768,2304]{1,0:T(8,128)(2,1)S(1)} %copy-done.1, bf16[768,2304]{1,0:T(8,128)(2,1)S(1)} %copy-done.1, ...), custom_call_target="tpu_custom_call" | custom-call | flops 20000000000 | bytes 20000000 | tf_op jit(solution)/shard_map/pallas_call | solution.py:138
  (2 shorter events, 0.0 us)
Async XLA Ops:
  7.2 42.2 %copy-start = (bf16[512,2048]{1,0:T(8,128)(2,1)S(1)}, bf16[512,2048]{1,0:T(8,128)(2,1)}, u32[]{:S(2)}) copy-start(bf16[512,2048]{1,0:T(8,128)(2,1)} %param.8) | copy-start | bytes 6291460
  9.8 13.7 %all-to-all-start = ((s32[16,32,1]{1,2,0:T(1,128)}), s32[16,32,1]{1,2,0:T(1,128)S(1)}, u32[]{:S(2)}, u32[]{:S(2)}) async-start(s32[16,32,1]{1,2,0:T(1,128)} %all_to_all.36), calls=%async_computation | async-start | bytes 16384 | tf_op jit(solution)/shard_map/all_to_all | solution.py:170
  23.6 10.3 %all-to-all-start.2 = ((bf16[256,2,384]{0,2,1:T(8,128)(2,1)}), bf16[256,2,384]{0,2,1:T(8,128)(2,1)S(1)}, u32[]{:S(2)}, u32[]{:S(2)}) async-start(bf16[256,2,384]{0,2,1:T(8,128)(2,1)} %bitcast.6), calls=%async_computation.2 | async-start | bytes 786432 | tf_op jit(solution)/shard_map/all_to_all | solution.py:173
  27.0 122.3 %all-reduce.2.cloned.1.call-start = ((), (), s32[]{:S(2)}) async-start(), calls=%async_computation.6 | async-start | bytes 3145728 | tf_op jit(solution)/shard_map/psum | solution.py:185
  51.5 137.3 %all-gather.6.cloned.1.call-start = ((), (), s32[]{:S(2)}) async-start(), calls=%async_computation.5 | async-start | bytes 1253376 | tf_op jit(solution)/shard_map/all_gather | solution.py:200
  52.3 185.1 %all-gather.4.cloned.1.call-start = ((), (), s32[]{:S(2)}) async-start(), calls=%async_computation.4 | async-start | bytes 3760128 | tf_op jit(solution)/shard_map/all_gather | solution.py:199
  53.0 7.6 %copy-start.3 = (f32[768]{0:T(1024)S(1)}, f32[768]{0:T(1024)}, u32[]{:S(2)}) copy-start(f32[768]{0:T(1024)} %param.13) | copy-start | bytes 9220
  56.4 19.2 %all-to-all-start.1 = ((bf16[16,32,384]{2,1,0:T(8,128)(2,1)}), bf16[16,32,384]{2,1,0:T(8,128)(2,1)S(1)}, u32[]{:S(2)}, u32[]{:S(2)}) async-start(bf16[16,32,384]{2,1,0:T(8,128)(2,1)} %bitcast.1), calls=%async_computation.1 | async-start | bytes 786432 | tf_op jit(solution)/shard_map/all_to_all | solution.py:188
  237.3 2.0 copy-start.1
  239.3 1.3 copy-start.2
Sparse Core Ops, SparseCore 0:
  51.6 97.6 all-reduce.1
  151.6 37.2 all-gather.5
  191.1 46.1 all-gather.3

commit v2 on v1

--- a/solution.py
+++ b/solution.py
@@ -17,6 +17,231 @@
 
 F32 = jnp.float32
 BF16 = jnp.bfloat16
+MESH = pl.DeviceIdType.MESH
+
+
+def greet(dp_peers, seq_peers):
+    barrier = pltpu.get_barrier_semaphore()
+    dp_count, seq_count = lax.axis_size("dp"), lax.axis_size("seq")
+    dp, seq = lax.axis_index("dp"), lax.axis_index("seq")
+    if dp_peers:
+
+        @pl.loop(1, dp_count)
+        def _(t):
+            pl.semaphore_signal(
+                barrier, device_id=(lax.rem(dp + t, dp_count), seq), device_id_type=MESH
+            )
+
+    if seq_peers:
+
+        @pl.loop(1, seq_count)
+        def _(t):
+            pl.semaphore_signal(
+                barrier, device_id=(dp, lax.rem(seq + t, seq_count)), device_id_type=MESH
+            )
+
+    pl.semaphore_wait(
+        barrier, (dp_count - 1 if dp_peers else 0) + (seq_count - 1 if seq_peers else 0)
+    )
+
+
+def remote(src, dst, send, recv, device):
+    return pltpu.make_async_remote_copy(
+        src_ref=src,
+        dst_ref=dst,
+        send_sem=send,
+        recv_sem=recv,
+        device_id=device,
+        device_id_type=MESH,
+    )
+
+
+def first_kernel(n, seq_count, pos, grad, pos_out, grad_out, ps, pr, gs, gr):
+    dp, seq = lax.axis_index("dp"), lax.axis_index("seq")
+    greet(True, True)
+
+    def grad_copy(t):
+        peer = lax.rem(seq + t, seq_count)
+        return remote(grad.at[peer], grad_out.at[seq], gs.at[t], gr.at[t], (dp, peer))
+
+    def pos_copy(t):
+        peer = lax.rem(dp + t, n)
+        return remote(pos.at[peer], pos_out.at[dp], ps.at[t], pr.at[t], (peer, seq))
+
+    @pl.loop(1, n)
+    def _(t):
+        pos_copy(t).start()
+
+    @pl.loop(1, seq_count)
+    def _(t):
+        grad_copy(t).start()
+
+    pos_out[dp] = pos[dp]
+    grad_out[seq] = grad[seq]
+
+    @pl.loop(1, n)
+    def _(t):
+        pos_copy(t).wait()
+
+    @pl.loop(1, seq_count)
+    def _(t):
+        grad_copy(t).wait()
+
+
+def second_kernel(n, seq_count, emb, grad, emb_out, grad_out, es, er, gs, gr, fs, fr):
+    dp, seq = lax.axis_index("dp"), lax.axis_index("seq")
+    greet(True, True)
+
+    def emb_copy(t):
+        peer = lax.rem(dp + t, n)
+        return remote(emb.at[peer], emb_out.at[seq, dp], es.at[t], er.at[t], (peer, seq))
+
+    def grad_copy(t):
+        peer = lax.rem(dp + t, n)
+        return remote(grad.at[peer], grad_out.at[dp], gs.at[t], gr.at[t], (peer, seq))
+
+    def forward(k, t):
+        source = lax.rem(dp - t + n, n)
+        peer = lax.rem(seq + k, seq_count)
+        block = emb_out.at[seq, source]
+        return remote(block, block, fs.at[k, t], fr.at[k, t], (dp, peer))
+
+    @pl.loop(1, n)
+    def _(t):
+        emb_copy(t).start()
+
+    @pl.loop(1, n)
+    def _(t):
+        grad_copy(t).start()
+
+    emb_out[seq, dp] = emb[dp]
+    grad_out[dp] = grad[dp]
+    for k in range(1, seq_count):
+        forward(k, 0).start()
+
+    @pl.loop(1, n)
+    def _(t):
+        emb_copy(t).wait_recv()
+        for k in range(1, seq_count):
+            forward(k, t).start()
+
+    @pl.loop(1, n)
+    def _(t):
+        grad_copy(t).wait()
+        emb_copy(t).wait_send()
+
+    @pl.loop(0, n)
+    def _(t):
+        for k in range(1, seq_count):
+            forward(k, t).wait()
+
+
+def reduce_kernel(
+    n, src, out, pair, stage, arrive, s1, r1, s2, r2, s3, r3, s4, r4
+):
+    dp, seq = lax.axis_index("dp"), lax.axis_index("seq")
+    half = n // 2
+    side, group = lax.rem(dp, 2), dp // 2
+    sibling = (group * 2 + 1 - side, seq)
+    barrier = pltpu.get_barrier_semaphore()
+    pl.semaphore_signal(barrier, device_id=sibling, device_id_type=MESH)
+
+    @pl.loop(1, half)
+    def _(t):
+        pl.semaphore_signal(
+            barrier,
+            device_id=(lax.rem(group + t, half) * 2 + side, seq),
+            device_id_type=MESH,
+        )
+
+    pl.semaphore_wait(barrier, half)
+
+    def ahead(t):
+        return lax.rem(group + t, half)
+
+    def behind(t):
+        return lax.rem(group - t + half, half)
+
+    def to_sibling(t):
+        return remote(src.at[1 - side, ahead(t)], pair.at[t], s1.at[t], r1.at[t], sibling)
+
+    def to_owner(t):
+        return remote(
+            stage.at[t], arrive.at[t], s2.at[t], r2.at[t], (ahead(t) * 2 + side, seq)
+        )
+
+    def to_peer(t):
+        block = out.at[side, group]
+        return remote(block, block, s3.at[t], r3.at[t], (ahead(t) * 2 + side, seq))
+
+    def hand_over(t):
+        block = out.at[side, behind(t)]
+        return remote(block, block, s4.at[t], r4.at[t], sibling)
+
+    @pl.loop(1, half)
+    def _(t):
+        to_sibling(t).start()
+
+    to_sibling(0).start()
+
+    @pl.loop(1, half)
+    def _(t):
+        to_sibling(t).wait_recv()
+        stage[t] = (src[side, ahead(t)].astype(F32) + pair[t].astype(F32)).astype(BF16)
+        to_owner(t).start()
+
+    to_sibling(0).wait_recv()
+    stage[0] = (src[side, group].astype(F32) + pair[0].astype(F32)).astype(BF16)
+
+    @pl.loop(1, half)
+    def _(t):
+        to_owner(t).wait_recv()
+
+    total = stage[0].astype(F32)
+    for t in range(1, half):
+        total = total + arrive[t].astype(F32)
+    out[side, group] = total.astype(BF16)
+
+    @pl.loop(1, half)
+    def _(t):
+        to_peer(t).start()
+
+    hand_over(0).start()
+
+    @pl.loop(1, half)
+    def _(t):
+        to_peer(t).wait_recv()
+        hand_over(t).start()
+
+    @pl.loop(1, half)
+    def _(t):
+        to_owner(t).wait_send()
+        to_peer(t).wait_send()
+
+    @pl.loop(0, half)
+    def _(t):
+        to_sibling(t).wait_send()
+        hand_over(t).wait()
+
+
+VM = pl.BlockSpec(memory_space=pltpu.VMEM)
+DMA = pltpu.SemaphoreType.DMA
+
+
+def exchange(kernel, ident, outs, scratch, *operands):
+    return pl.pallas_call(
+        kernel,
+        out_shape=tuple(jax.ShapeDtypeStruct(shape, kind) for shape, kind in outs),
+        in_specs=[VM] * len(operands),
+        out_specs=tuple([VM] * len(outs)),
+        scratch_shapes=scratch,
+        compiler_params=pltpu.CompilerParams(
+            collective_id=ident, has_side_effects=True, vmem_limit_bytes=32 * 1024 * 1024
+        ),
+        cost_estimate=pl.CostEstimate(
+            flops=10_000_000_000, bytes_accessed=10_000_000, transcendentals=0
+        ),
+    )(*operands)
 
 
 def put_rows(whole, rows, low, high):
@@ -129,7 +354,7 @@
         branch_ref[...] = jnp.dot(whole, wo_ref[...], preferred_element_type=F32).astype(BF16)
 
 
-def attend(meta, rows, gain, w_qkv, w_out, seq_count, nearby):
+def attend(meta, rows, gain, weights, seq_count, nearby):
     width = STEP_HEADS * HEAD_WIDTH
     steps = HEAD_COUNT // STEP_HEADS
     slide_len = rows.shape[1]
@@ -146,7 +371,7 @@
             pl.BlockSpec((D, width), lambda i: (0, i)),
             pl.BlockSpec((D, width), lambda i: (0, steps + i)),
             pl.BlockSpec((D, width), lambda i: (0, 2 * steps + i)),
-            full(D, D),
+            pl.BlockSpec((D, D), lambda i: (0, 3)),
         ],
         out_specs=(full(nearby, D), full(nearby, D)),
         scratch_shapes=[
@@ -157,49 +382,78 @@
         cost_estimate=pl.CostEstimate(
             flops=20_000_000_000, bytes_accessed=20_000_000, transcendentals=1_000_000
         ),
-    )(meta, rows, gain, w_qkv, w_qkv, w_qkv, w_out)
+    )(meta, rows, gain, weights, weights, weights, weights)
 
 
 def local(tile_feats, tile_pos, slide_count, w_proj, emb_grad, ln_gain, w_qkv, w_out):
     seq_count = lax.axis_size("seq")
+    n = lax.axis_size("dp")
     seq_index = lax.axis_index("seq")
     slot_rows = tile_feats.shape[0]
     nearby = emb_grad.shape[1]
     slide_len = nearby * seq_count
     part = nearby // DILATION_STEP
-    positions = lax.all_to_all(
-        tile_pos.reshape(slot_rows), "dp", split_axis=0, concat_axis=0, tiled=True
-    )
-    returned_grad = lax.all_to_all(
-        emb_grad.reshape(nearby, D), "seq", split_axis=1, concat_axis=0, tiled=True
-    )
+    most = slot_rows // n
+    width = w_proj.shape[1]
+    weights = lax.all_gather(
+        jnp.concatenate([w_qkv, w_out], axis=1), "dp", axis=0, tiled=True
+    )
+    positions, returned_grad = exchange(
+        functools.partial(first_kernel, n, seq_count),
+        1,
+        [((n, 1, most), jnp.int32), ((seq_count, nearby, width), BF16)],
+        [DMA((n,)), DMA((n,)), DMA((seq_count,)), DMA((seq_count,))],
+        tile_pos.reshape(n, 1, most),
+        emb_grad.reshape(nearby, seq_count, width).transpose(1, 0, 2),
+    )
+    positions = positions.reshape(slot_rows)
     spot = jnp.arange(slide_len, dtype=jnp.int32)
     hot = (spot[:, None] == positions[None, :]).astype(BF16)
     picked_grad = lax.dot_general(
-        hot, returned_grad, (((0,), (0,)), ((), ())), preferred_element_type=F32
+        hot,
+        returned_grad.reshape(slide_len, width),
+        (((0,), (0,)), ((), ())),
+        preferred_element_type=F32,
     ).astype(BF16)
-    slot_grad = lax.all_to_all(picked_grad, "dp", split_axis=0, concat_axis=0, tiled=True)
+    emb_part = jnp.dot(tile_feats, w_proj, preferred_element_type=F32).astype(BF16)
+    arrived, slot_grad = exchange(
+        functools.partial(second_kernel, n, seq_count),
+        2,
+        [((seq_count, n, most, width), BF16), ((n, most, width), BF16)],
+        [DMA((n,))] * 4 + [DMA((seq_count, n))] * 2,
+        emb_part.reshape(n, most, width),
+        picked_grad.reshape(n, most, width),
+    )
     grad_part = lax.dot_general(
-        tile_feats, slot_grad, (((0,), (0,)), ((), ())), preferred_element_type=F32
-    )
-    proj_grad = lax.psum(grad_part.astype(BF16), "dp").astype(F32)
-
-    emb_part = jnp.dot(tile_feats, w_proj, preferred_element_type=F32).astype(BF16)
-    arrived = lax.all_to_all(emb_part, "dp", split_axis=0, concat_axis=0, tiled=True)
+        tile_feats,
+        slot_grad.reshape(slot_rows, width),
+        (((0,), (0,)), ((), ())),
+        preferred_element_type=F32,
+    ).astype(BF16)
+    features = grad_part.shape[0]
+    half = n // 2
+    shape = (2, half, features // n, width)
+    (summed,) = exchange(
+        functools.partial(reduce_kernel, n),
+        3,
+        [(shape, BF16)],
+        [pltpu.VMEM(shape[1:], BF16)] * 3 + [DMA((half,))] * 8,
+        grad_part.reshape(shape),
+    )
+    proj_grad = summed.reshape(features, width).astype(F32)
+
     inside = spot % nearby
     at_spot = spot - inside + (inside % part) * DILATION_STEP + inside // part
     hot_perm = (at_spot[:, None] == positions[None, :]).astype(BF16)
-    slide_rows = jnp.dot(hot_perm, arrived, preferred_element_type=F32).astype(BF16)
-    rows = lax.all_gather(slide_rows, "seq", axis=0, tiled=False)
+    rows = jnp.einsum(
+        "ps,csw->cpw",
+        hot_perm,
+        arrived.reshape(seq_count, slot_rows, width),
+        preferred_element_type=F32,
+    ).astype(BF16)
     meta = jnp.stack([seq_index.astype(jnp.int32), slide_count[0]])
     local_emb, attn_branch = attend(
-        meta,
-        rows,
-        ln_gain.reshape(1, D),
-        lax.all_gather(w_qkv, "dp", axis=0, tiled=True),
-        lax.all_gather(w_out, "dp", axis=0, tiled=True),
-        seq_count,
-        nearby,
+        meta, rows, ln_gain.reshape(1, D), weights, seq_count, nearby
     )
     return (local_emb[None], attn_branch[None], proj_grad)
 

time: 258 us -> 131 us (0.51)
  the two profiles are of different devices: /device:TPU:0 before, /device:TPU:27 now
where the time goes in v2:
time: 131 us
  Pallas kernels  96.4 us (74%)
  between operations  14.8 us (11%)
  local copies, waits for them, and re-layouts  7.05 us (5%)
  matrix products  6.8 us (5%)
  other arithmetic  5.97 us (5%)
    pallas_call x3, Pallas kernels, exchange(): pl.pallas_call(kernel, out_shape=tuple((jax.ShapeDtypeStruct(shape, kind)...  86 us
    pallas_call x1, Pallas kernels, attend(): pl.pallas_call(functools.partial(attention_kernel, seq_count, nearby), ou...  10.4 us
    unnamed x12, local copies, waits for them, and re-layouts  4.04 us
    dot_general x1, matrix products, local(): jnp.dot(tile_feats, w_proj, preferred_element_type=F32).astype(BF16)  2.65 us
    convert_element_type x1, local copies, waits for them, and re-layouts, local(): grad_part = lax.dot_general(tile_feats, slot_grad.reshape(slot_rows, widt...  2.62 us
  transfers between devices with their start and end apart: 1, of which 0 were waited for; matrix products, arithmetic and copies ran while one was open for 12% of the time, Pallas kernels for 66%

profile of v2, /device:TPU:27, one launch (start us, length us, event | category | flops | bytes accessed | tf_op | source)
XLA Modules:
  0.0 131.1 jit_solution(2169736982681327751)
XLA Ops:
  7.2 0.0 copy-start
  7.2 0.0 all-gather.2.cloned.1.call-start
  7.2 1.8 %pad_maximum_fusion = bf16[48,3072]{1,0:T(8,128)(2,1)} fusion(bf16[48,768]{1,0:T(8,128)(2,1)} %param.15, bf16[48,2304]{1,0:T(8,128)(2,1)} %param.14), kind=kLoop, calls=%fused_computation.13 | loop fusion | flops 589824 | bytes 589824 | tf_op jit(solution)/shard_map/concatenate | solution.py:399
  9.1 0.0 all-gather.2.cloned.1.call-update
  9.1 0.5 broadcast.83
  9.6 1.3 %reduce.6 = s32[512]{0:T(512)S(1)} reduce(s32[1,512]{1,0:T(1,128)} %param.9, s32[]{:T(128)} %broadcast.83), dimensions={0}, to_apply=%param.9.reduce_sub_computation.3 | reduce | bytes 4100 | tf_op args[1]
  11.0 0.1 reshape.78.pos
  11.0 1.2 copy.14
  12.2 0.2 copy.15
  12.4 0.0 copy-start.4
  12.4 7.6 %shard_map.103 = (s32[16,1,32]{2,1,0:T(1,128)S(1)}, bf16[2,256,384]{2,1,0:T(8,128)(2,1)S(1)}) custom-call(s32[16,1,32]{2,1,0:T(1,128)S(1)} %reshape.78.pos, bf16[2,256,384]{2,1,0:T(8,128)(2,1)S(1)} %bitcast.28), custom_call_target="tpu_custom_call" | custom-call | flops 10000000000 | bytes 10000000 | tf_op jit(solution)/shard_map/pallas_call | solution.py:232
  20.1 0.7 reduce.7
  20.8 0.1 eq.30
  20.9 0.0 copy-done.4
  21.5 0.5 convolution_convert_fusion.3
  22.0 0.0 copy-done
  22.0 2.7 %convolution_convert_fusion.2 = bf16[512,384]{1,0:T(8,128)(2,1)S(1)} fusion(bf16[512,2048]{1,0:T(8,128)(2,1)S(1)} %copy-done, bf16[2048,384]{1,0:T(8,128)(2,1)} %param.11), kind=kOutput, calls=%fused_computation.5 | convolution fusion | flops 805502976 | bytes 4063232 | tf_op jit(solution)/shard_map/dot_general | solution.py:418
  24.7 33.9 %shard_map.104 = (bf16[2,16,32,384]{3,2,1,0:T(8,128)(2,1)S(1)}, bf16[16,32,384]{2,1,0:T(8,128)(2,1)S(1)}) custom-call(bf16[16,32,384]{2,1,0:T(8,128)(2,1)S(1)} %bitcast.33, bf16[16,32,384]{2,1,0:T(8,128)(2,1)S(1)} %bitcast.32), custom_call_target="tpu_custom_call" | custom-call | flops 10000000000 | bytes 10000000 | tf_op jit(solution)/shard_map/pallas_call | solution.py:232
  58.6 2.2 %fusion = bf16[2048,384]{0,1:T(8,128)(2,1)} fusion(bf16[512,384]{1,0:T(8,128)(2,1)S(1)} %bitcast.29, bf16[512,2048]{1,0:T(8,128)(2,1)S(1)} %copy-done), kind=kOutput, calls=%fused_computation.1 | convolution fusion | flops 806092800 | bytes 4063232 | tf_op jit(solution)/shard_map/dot_general | solution.py:427
  60.7 2.6 %copy.18 = bf16[2048,384]{1,0:T(8,128)(2,1)} copy(bf16[2048,384]{0,1:T(8,128)(2,1)} %fusion) | data formatting | bytes 3145728 | tf_op jit(solution)/shard_map/convert_element_type | solution.py:432
  63.3 0.0 copy-start.1
  63.3 0.1 pad_add_fusion.meta_ref
  63.4 1.5 %fusion.1.rows_ref = bf16[2,512,384]{2,1,0:T(8,128)(2,1)} fusion(bf16[2,512,384]{2,1,0:T(8,128)(2,1)S(1)} %bitcast.30, s32[512]{0:T(512)S(1)} %eq.30, s32[512]{0:T(512)S(1)} %fusion.13), kind=kOutput, calls=%fused_computation.4 | convolution fusion | flops 403308544 | bytes 1576960 | tf_op jit(solution)/shard_map/ps,csw->cpw/dot_general | solution.py:448
  64.9 0.0 copy-done.1
  64.9 44.5 %shard_map.106 = bf16[2,8,128,384]{3,2,1,0:T(8,128)(2,1)S(1)} custom-call(bf16[2,8,128,384]{3,2,1,0:T(8,128)(2,1)S(1)} %bitcast.27), custom_call_target="tpu_custom_call" | custom-call | flops 10000000000 | bytes 10000000 | tf_op jit(solution)/shard_map/pallas_call | solution.py:232
  109.4 0.0 copy-start.3
  109.5 2.0 %bitcast_convert_fusion = f32[2048,384]{1,0:T(8,128)} fusion(bf16[2,8,128,384]{3,2,1,0:T(8,128)(2,1)S(1)} %shard_map.106), kind=kLoop, calls=%fused_computation.2 | loop fusion | flops 786432 | bytes 4718592 | tf_op jit(solution)/shard_map/convert_element_type | solution.py:443
  111.5 0.0 all-gather.2.cloned.1.call-done.wq_ref.wk_ref.wv_ref.wo_ref
  111.5 0.0 copy-done.3
  111.5 0.0 copy-start.2
  111.5 2.3 %copy-done.2 = bf16[768,3072]{1,0:T(8,128)(2,1)S(1)} copy-done((bf16[768,3072]{1,0:T(8,128)(2,1)S(1)}, bf16[768,3072]{1,0:T(8,128)(2,1)}, u32[]{:S(2)}) %copy-start.2) | copy-done | bytes 4718616
  113.8 10.4 %shard_map.105 = (bf16[256,768]{1,0:T(8,128)(2,1)}, bf16[256,768]{1,0:T(8,128)(2,1)}) custom-call(s32[2]{0:T(128)S(1)} %pad_add_fusion.meta_ref, bf16[2,512,384]{2,1,0:T(8,128)(2,1)S(1)} %copy-done.3, f32[1,768]{1,0:T(1,128)S(1)} %reshape.83.gain_ref, bf16[768,3072]{1,0:T(8,128)(2,1)S(1)} %copy-done.2, bf16[768,3072]{1,0:T(8,128)(2,1)S(1)} %copy-done.2, ...), custom_call_target="tpu_custom_call" | custom-call | flops 20000000000 | bytes 20000000 | tf_op jit(solution)/shard_map/pallas_call | solution.py:363
  (2 shorter events, 0.0 us)
Async XLA Ops:
  7.2 14.9 %copy-start = (bf16[512,2048]{1,0:T(8,128)(2,1)S(1)}, bf16[512,2048]{1,0:T(8,128)(2,1)}, u32[]{:S(2)}) copy-start(bf16[512,2048]{1,0:T(8,128)(2,1)} %param.8) | copy-start | bytes 6291460
  7.2 104.3 %all-gather.2.cloned.1.call-start = ((), (), s32[]{:S(2)}) async-start(), calls=%async_computation | async-start | bytes 5013504 | tf_op jit(solution)/shard_map/all_gather | solution.py:398
  12.4 8.4 %copy-start.4 = (f32[768]{0:T(1024)S(1)}, f32[768]{0:T(1024)}, u32[]{:S(2)}) copy-start(f32[768]{0:T(1024)} %param.13) | copy-start | bytes 9220
  63.3 1.6 %copy-start.1 = (bf16[2048,384]{1,0:T(8,128)(2,1)S(1)}, bf16[2048,384]{1,0:T(8,128)(2,1)}, u32[]{:S(2)}) copy-start(bf16[2048,384]{1,0:T(8,128)(2,1)} %copy.18) | copy-start | bytes 4718596
  109.4 2.0 %copy-start.3 = (bf16[2,512,384]{2,1,0:T(8,128)(2,1)S(1)}, bf16[2,512,384]{2,1,0:T(8,128)(2,1)}, u32[]{:S(2)}) copy-start(bf16[2,512,384]{2,1,0:T(8,128)(2,1)} %fusion.1.rows_ref) | copy-start | bytes 2359300
  111.5 2.3 %copy-start.2 = (bf16[768,3072]{1,0:T(8,128)(2,1)S(1)}, bf16[768,3072]{1,0:T(8,128)(2,1)}, u32[]{:S(2)}) copy-start(bf16[768,3072]{1,0:T(8,128)(2,1)} %all-gather.2.cloned.1.call-done.wq_ref.wk_ref.wv_ref.wo_ref) | copy-start | bytes 14155780
Sparse Core Ops, SparseCore 0:
  10.9 59.6 all-gather.1

commit v3 on v2

--- a/solution.py
+++ b/solution.py
@@ -56,49 +56,30 @@
     )
 
 
-def first_kernel(n, seq_count, pos, grad, pos_out, grad_out, ps, pr, gs, gr):
+def dispatch_kernel(
+    n, seq_count, pos, grad, emb, pos_out, emb_out, grad_out, grad_rows, picked, *sems
+):
+    ps, pr, xs, xr, es, er, gs, gr, fs, fr = sems
     dp, seq = lax.axis_index("dp"), lax.axis_index("seq")
+    most = pos.shape[2]
+    nearby, width = grad.shape[1:]
     greet(True, True)
 
-    def grad_copy(t):
+    def column_copy(t):
         peer = lax.rem(seq + t, seq_count)
-        return remote(grad.at[peer], grad_out.at[seq], gs.at[t], gr.at[t], (dp, peer))
+        return remote(grad.at[peer], grad_rows.at[seq], xs.at[t], xr.at[t], (dp, peer))
 
     def pos_copy(t):
         peer = lax.rem(dp + t, n)
         return remote(pos.at[peer], pos_out.at[dp], ps.at[t], pr.at[t], (peer, seq))
 
-    @pl.loop(1, n)
-    def _(t):
-        pos_copy(t).start()
-
-    @pl.loop(1, seq_count)
-    def _(t):
-        grad_copy(t).start()
-
-    pos_out[dp] = pos[dp]
-    grad_out[seq] = grad[seq]
-
-    @pl.loop(1, n)
-    def _(t):
-        pos_copy(t).wait()
-
-    @pl.loop(1, seq_count)
-    def _(t):
-        grad_copy(t).wait()
-
-
-def second_kernel(n, seq_count, emb, grad, emb_out, grad_out, es, er, gs, gr, fs, fr):
-    dp, seq = lax.axis_index("dp"), lax.axis_index("seq")
-    greet(True, True)
-
     def emb_copy(t):
         peer = lax.rem(dp + t, n)
         return remote(emb.at[peer], emb_out.at[seq, dp], es.at[t], er.at[t], (peer, seq))
 
     def grad_copy(t):
         peer = lax.rem(dp + t, n)
-        return remote(grad.at[peer], grad_out.at[dp], gs.at[t], gr.at[t], (peer, seq))
+        return remote(picked.at[peer], grad_out.at[dp], gs.at[t], gr.at[t], (peer, seq))
 
     def forward(k, t):
         source = lax.rem(dp - t + n, n)
@@ -106,16 +87,47 @@
         block = emb_out.at[seq, source]
         return remote(block, block, fs.at[k, t], fr.at[k, t], (dp, peer))
 
+    @pl.loop(1, seq_count)
+    def _(t):
+        column_copy(t).start()
+
     @pl.loop(1, n)
     def _(t):
+        pos_copy(t).start()
+
+    @pl.loop(1, n)
+    def _(t):
         emb_copy(t).start()
 
+    pos_out[dp] = pos[dp]
+    grad_rows[seq] = grad[seq]
+    emb_out[seq, dp] = emb[dp]
+
     @pl.loop(1, n)
     def _(t):
+        pos_copy(t).wait()
+
+    @pl.loop(1, seq_count)
+    def _(t):
+        column_copy(t).wait()
+
+    rows = jnp.concatenate([grad_rows[i] for i in range(seq_count)], axis=0)
+    spot = lax.broadcasted_iota(jnp.int32, (nearby * seq_count, 1), 0)
+    batch = 4
+    for first in range(0, n, batch):
+        at = jnp.concatenate([pos_out[first + i] for i in range(batch)], axis=1)
+        hot = jnp.where(spot == at, 1.0, 0.0).astype(BF16)
+        block = lax.dot_general(
+            hot, rows, (((0,), (0,)), ((), ())), preferred_element_type=F32
+        ).astype(BF16)
+        for i in range(batch):
+            picked[first + i] = block[i * most : (i + 1) * most]
+
+    @pl.loop(1, n)
+    def _(t):
         grad_copy(t).start()
 
-    emb_out[seq, dp] = emb[dp]
-    grad_out[dp] = grad[dp]
+    grad_out[dp] = picked[dp]
     for k in range(1, seq_count):
         forward(k, 0).start()
 
@@ -127,8 +139,8 @@
 
     @pl.loop(1, n)
     def _(t):
+        emb_copy(t).wait_send()
         grad_copy(t).wait()
-        emb_copy(t).wait_send()
 
     @pl.loop(0, n)
     def _(t):
@@ -136,92 +148,124 @@
             forward(k, t).wait()
 
 
-def reduce_kernel(
-    n, src, out, pair, stage, arrive, s1, r1, s2, r2, s3, r3, s4, r4
-):
+def reduce_kernel(n, src, out, pair, cross, stage_b, stage_c, arrive, *sems):
+    s1, r1, s2, r2, s3, r3, s4, r4, s5, r5, s6, r6 = sems
     dp, seq = lax.axis_index("dp"), lax.axis_index("seq")
-    half = n // 2
-    side, group = lax.rem(dp, 2), dp // 2
-    sibling = (group * 2 + 1 - side, seq)
+    q = n // 4
+    a, b, c = lax.rem(dp, 2), lax.rem(dp // 2, 2), dp // 4
+    sibling = (dp + 1 - 2 * a, seq)
+    across = (dp + 2 - 4 * b, seq)
     barrier = pltpu.get_barrier_semaphore()
     pl.semaphore_signal(barrier, device_id=sibling, device_id_type=MESH)
-
-    @pl.loop(1, half)
-    def _(t):
-        pl.semaphore_signal(
-            barrier,
-            device_id=(lax.rem(group + t, half) * 2 + side, seq),
-            device_id_type=MESH,
+    pl.semaphore_signal(barrier, device_id=across, device_id_type=MESH)
+
+    def ahead(t):
+        return lax.rem(c + t, q)
+
+    def behind(t):
+        return lax.rem(c - t + q, q)
+
+    def along(t):
+        return (ahead(t) * 4 + b * 2 + a, seq)
+
+    @pl.loop(1, q)
+    def _(t):
+        pl.semaphore_signal(barrier, device_id=along(t), device_id_type=MESH)
+
+    pl.semaphore_wait(barrier, q + 1)
+
+    def side(i):
+        return 1 - b if i == 0 else b
+
+    def to_sibling(i, t):
+        return remote(
+            src.at[1 - a, side(i), ahead(t)], pair.at[i, t], s1.at[i, t], r1.at[i, t], sibling
         )
 
-    pl.semaphore_wait(barrier, half)
-
-    def ahead(t):
-        return lax.rem(group + t, half)
-
-    def behind(t):
-        return lax.rem(group - t + half, half)
-
-    def to_sibling(t):
-        return remote(src.at[1 - side, ahead(t)], pair.at[t], s1.at[t], r1.at[t], sibling)
+    def to_across(t):
+        return remote(stage_b.at[t], cross.at[t], s2.at[t], r2.at[t], across)
 
     def to_owner(t):
-        return remote(
-            stage.at[t], arrive.at[t], s2.at[t], r2.at[t], (ahead(t) * 2 + side, seq)
-        )
-
-    def to_peer(t):
-        block = out.at[side, group]
-        return remote(block, block, s3.at[t], r3.at[t], (ahead(t) * 2 + side, seq))
-
-    def hand_over(t):
-        block = out.at[side, behind(t)]
-        return remote(block, block, s4.at[t], r4.at[t], sibling)
-
-    @pl.loop(1, half)
-    def _(t):
-        to_sibling(t).start()
-
-    to_sibling(0).start()
-
-    @pl.loop(1, half)
-    def _(t):
-        to_sibling(t).wait_recv()
-        stage[t] = (src[side, ahead(t)].astype(F32) + pair[t].astype(F32)).astype(BF16)
-        to_owner(t).start()
-
-    to_sibling(0).wait_recv()
-    stage[0] = (src[side, group].astype(F32) + pair[0].astype(F32)).astype(BF16)
-
-    @pl.loop(1, half)
-    def _(t):
+        return remote(stage_c.at[t], arrive.at[t], s3.at[t], r3.at[t], along(t))
+
+    def result_along(t):
+        block = out.at[a, b, c]
+        return remote(block, block, s4.at[t], r4.at[t], along(t))
+
+    def result_across(t):
+        block = out.at[a, b, behind(t)]
+        return remote(block, block, s5.at[t], r5.at[t], across)
+
+    def result_sibling(i, t):
+        block = out.at[a, side(i), behind(t)]
+        return remote(block, block, s6.at[i, t], r6.at[i, t], sibling)
+
+    for i in (0, 1):
+
+        @pl.loop(1, q + 1)
+        def _(t):
+            to_sibling(i, lax.rem(t, q)).start()
+
+    @pl.loop(1, q + 1)
+    def _(step):
+        t = lax.rem(step, q)
+        to_sibling(0, t).wait_recv()
+        stage_b[t] = (src[a, 1 - b, ahead(t)].astype(F32) + pair[0, t].astype(F32)).astype(BF16)
+        to_across(t).start()
+
+    @pl.loop(1, q + 1)
+    def _(step):
+        t = lax.rem(step, q)
+        to_sibling(1, t).wait_recv()
+        to_across(t).wait_recv()
+        stage_c[t] = (
+            src[a, b, ahead(t)].astype(F32) + pair[1, t].astype(F32) + cross[t].astype(F32)
+        ).astype(BF16)
+
+        @pl.when(step < q)
+        def _():
+            to_owner(t).start()
+
+    total = stage_c[0].astype(F32)
+    for t in range(1, q):
         to_owner(t).wait_recv()
-
-    total = stage[0].astype(F32)
-    for t in range(1, half):
         total = total + arrive[t].astype(F32)
-    out[side, group] = total.astype(BF16)
-
-    @pl.loop(1, half)
-    def _(t):
-        to_peer(t).start()
-
-    hand_over(0).start()
-
-    @pl.loop(1, half)
-    def _(t):
-        to_peer(t).wait_recv()
-        hand_over(t).start()
-
-    @pl.loop(1, half)
+    out[a, b, c] = total.astype(BF16)
+
+    @pl.loop(1, q)
+    def _(t):
+        result_along(t).start()
+
+    result_across(0).start()
+    result_sibling(1, 0).start()
+
+    @pl.loop(1, q)
+    def _(t):
+        result_along(t).wait_recv()
+        result_across(t).start()
+        result_sibling(1, t).start()
+
+    @pl.loop(0, q)
+    def _(t):
+        result_across(t).wait_recv()
+        result_sibling(0, t).start()
+
+    @pl.loop(1, q)
     def _(t):
         to_owner(t).wait_send()
-        to_peer(t).wait_send()
-
-    @pl.loop(0, half)
-    def _(t):
-        to_sibling(t).wait_send()
-        hand_over(t).wait()
+        result_along(t).wait_send()
+
+    for i in (0, 1):
+
+        @pl.loop(0, q)
+        def _(t):
+            to_sibling(i, t).wait_send()
+            result_sibling(i, t).wait()
+
+    @pl.loop(0, q)
+    def _(t):
+        to_across(t).wait_send()
+        result_across(t).wait_send()
 
 
 VM = pl.BlockSpec(memory_space=pltpu.VMEM)
@@ -398,32 +442,26 @@
     weights = lax.all_gather(
         jnp.concatenate([w_qkv, w_out], axis=1), "dp", axis=0, tiled=True
     )
-    positions, returned_grad = exchange(
-        functools.partial(first_kernel, n, seq_count),
+    emb_part = jnp.dot(tile_feats, w_proj, preferred_element_type=F32).astype(BF16)
+    positions, arrived, slot_grad = exchange(
+        functools.partial(dispatch_kernel, n, seq_count),
         1,
-        [((n, 1, most), jnp.int32), ((seq_count, nearby, width), BF16)],
-        [DMA((n,)), DMA((n,)), DMA((seq_count,)), DMA((seq_count,))],
+        [
+            ((n, 1, most), jnp.int32),
+            ((seq_count, n, most, width), BF16),
+            ((n, most, width), BF16),
+        ],
+        [pltpu.VMEM((seq_count, nearby, width), BF16), pltpu.VMEM((n, most, width), BF16)]
+        + [DMA((n,))] * 2
+        + [DMA((seq_count,))] * 2
+        + [DMA((n,))] * 4
+        + [DMA((seq_count, n))] * 2,
         tile_pos.reshape(n, 1, most),
         emb_grad.reshape(nearby, seq_count, width).transpose(1, 0, 2),
+        emb_part.reshape(n, most, width),
     )
     positions = positions.reshape(slot_rows)
     spot = jnp.arange(slide_len, dtype=jnp.int32)
-    hot = (spot[:, None] == positions[None, :]).astype(BF16)
-    picked_grad = lax.dot_general(
-        hot,
-        returned_grad.reshape(slide_len, width),
-        (((0,), (0,)), ((), ())),
-        preferred_element_type=F32,
-    ).astype(BF16)
-    emb_part = jnp.dot(tile_feats, w_proj, preferred_element_type=F32).astype(BF16)
-    arrived, slot_grad = exchange(
-        functools.partial(second_kernel, n, seq_count),
-        2,
-        [((seq_count, n, most, width), BF16), ((n, most, width), BF16)],
-        [DMA((n,))] * 4 + [DMA((seq_count, n))] * 2,
-        emb_part.reshape(n, most, width),
-        picked_grad.reshape(n, most, width),
-    )
     grad_part = lax.dot_general(
         tile_feats,
         slot_grad.reshape(slot_rows, width),
@@ -431,13 +469,17 @@
         preferred_element_type=F32,
     ).astype(BF16)
     features = grad_part.shape[0]
-    half = n // 2
-    shape = (2, half, features // n, width)
+    quarter = n // 4
+    shape = (2, 2, quarter, features // n, width)
     (summed,) = exchange(
         functools.partial(reduce_kernel, n),
         3,
         [(shape, BF16)],
-        [pltpu.VMEM(shape[1:], BF16)] * 3 + [DMA((half,))] * 8,
+        [pltpu.VMEM(shape[1:], BF16)]
+        + [pltpu.VMEM(shape[2:], BF16)] * 4
+        + [DMA((2, quarter))] * 2
+        + [DMA((quarter,))] * 8
+        + [DMA((2, quarter))] * 2,
         grad_part.reshape(shape),
     )
     proj_grad = summed.reshape(features, width).astype(F32)

time: 131 us -> 124 us (0.947)
  the two profiles are of different devices: /device:TPU:27 before, /device:TPU:0 now
where the time goes in v3:
time: 124 us; the launch traced here: 122 us
  Pallas kernels  86.3 us (70%)
  between operations  14.8 us (12%)
  local copies, waits for them, and re-layouts  8.32 us (7%)
  matrix products  6.33 us (5%)
  other arithmetic  5.97 us (5%)
    pallas_call x2, Pallas kernels, exchange(): pl.pallas_call(kernel, out_shape=tuple((jax.ShapeDtypeStruct(shape, kind)...  75.9 us
    pallas_call x1, Pallas kernels, attend(): pl.pallas_call(functools.partial(attention_kernel, seq_count, nearby), ou...  10.4 us
    unnamed x16, local copies, waits for them, and re-layouts  4.93 us
    convert_element_type x1, local copies, waits for them, and re-layouts, local(): grad_part = lax.dot_general(tile_feats, slot_grad.reshape(slot_rows, widt...  3.01 us
    dot_general x1, matrix products, local(): jnp.dot(tile_feats, w_proj, preferred_element_type=F32).astype(BF16)  2.66 us
  transfers between devices with their start and end apart: 1, of which 0 were waited for; matrix products, arithmetic and copies ran while one was open for 13% of the time, Pallas kernels for 62%

profile of v3, /device:TPU:0, one launch (start us, length us, event | category | flops | bytes accessed | tf_op | source)
XLA Modules:
  0.0 121.7 jit_solution(12945214898228521161)
XLA Ops:
  7.2 0.0 copy-start
  7.2 0.0 all-gather.2.cloned.1.call-start
  7.2 1.8 %pad_maximum_fusion = bf16[48,3072]{1,0:T(8,128)(2,1)} fusion(bf16[48,768]{1,0:T(8,128)(2,1)} %param.15, bf16[48,2304]{1,0:T(8,128)(2,1)} %param.14), kind=kLoop, calls=%fused_computation.10 | loop fusion | flops 589824 | bytes 589824 | tf_op jit(solution)/shard_map/concatenate | solution.py:443
  9.1 0.0 all-gather.2.cloned.1.call-update
  9.1 0.5 broadcast.83
  9.6 1.3 %reduce.6 = s32[512]{0:T(512)S(1)} reduce(s32[1,512]{1,0:T(1,128)} %param.9, s32[]{:T(128)} %broadcast.83), dimensions={0}, to_apply=%param.9.reduce_sub_computation.3 | reduce | bytes 4100 | tf_op args[1]
  11.0 0.1 reshape.71.pos
  11.0 1.2 copy.14
  12.2 0.2 copy.15
  12.4 0.0 copy-done
  12.4 2.7 %convolution_convert_fusion.2 = bf16[512,384]{1,0:T(8,128)(2,1)S(1)} fusion(bf16[512,2048]{1,0:T(8,128)(2,1)S(1)} %copy-done, bf16[2048,384]{1,0:T(8,128)(2,1)} %param.11), kind=kOutput, calls=%fused_computation.5 | convolution fusion | flops 805502976 | bytes 4063232 | tf_op jit(solution)/shard_map/dot_general | solution.py:445
  15.1 0.0 copy-start.6
  15.1 32.7 %shard_map.103 = (s32[16,1,32]{2,1,0:T(1,128)S(1)}, bf16[2,16,32,384]{3,2,1,0:T(8,128)(2,1)S(1)}, bf16[16,32,384]{2,1,0:T(8,128)(2,1)S(1)}) custom-call(s32[16,1,32]{2,1,0:T(1,128)S(1)} %reshape.71.pos, bf16[2,256,384]{2,1,0:T(8,128)(2,1)S(1)} %bitcast.25, bf16[16,32,384]{2,1,0:T(8,128)(2,1)S(1)} %bitcast.28), custom_call_target="tpu_custom_call" | custom-call | flops 10000000000 | bytes 10000000 | tf_op jit(solution)/shard_map/pallas_call | solution.py:276
  47.8 0.0 copy-start.3
  47.9 0.9 copy-done.3
  48.7 0.7 reduce.7
  49.4 0.1 eq.19
  49.5 0.0 copy-done.6
  50.2 2.2 %fusion = bf16[2048,384]{0,1:T(8,128)(2,1)} fusion(bf16[512,384]{1,0:T(8,128)(2,1)S(1)} %bitcast.26, bf16[512,2048]{1,0:T(8,128)(2,1)S(1)} %copy-done), kind=kOutput, calls=%fused_computation.1 | convolution fusion | flops 806092800 | bytes 4063232 | tf_op jit(solution)/shard_map/dot_general | solution.py:465
  52.3 0.0 copy-start.4
  52.3 3.0 %copy.18 = bf16[2048,384]{1,0:T(8,128)(2,1)} copy(bf16[2048,384]{0,1:T(8,128)(2,1)} %fusion) | data formatting | bytes 3145728 | tf_op jit(solution)/shard_map/convert_element_type | solution.py:470
  55.3 0.0 copy-start.1
  55.3 0.1 pad_add_fusion.meta_ref
  55.4 0.0 copy-done.4
  55.4 1.5 %fusion.1.rows_ref = bf16[2,512,384]{2,1,0:T(8,128)(2,1)} fusion(bf16[2,512,384]{2,1,0:T(8,128)(2,1)S(1)} %bitcast.27, s32[512]{0:T(512)S(1)} %eq.19, s32[512]{0:T(512)S(1)} %fusion.12), kind=kOutput, calls=%fused_computation.4 | convolution fusion | flops 403308544 | bytes 1576960 | tf_op jit(solution)/shard_map/ps,csw->cpw/dot_general | solution.py:490
  56.9 0.0 copy-done.1
  56.9 43.2 %shard_map.105 = bf16[2,2,4,128,384]{4,3,2,1,0:T(8,128)(2,1)S(1)} custom-call(bf16[2,2,4,128,384]{4,3,2,1,0:T(8,128)(2,1)S(1)} %bitcast.24), custom_call_target="tpu_custom_call" | custom-call | flops 10000000000 | bytes 10000000 | tf_op jit(solution)/shard_map/pallas_call | solution.py:276
  100.1 0.0 copy-start.5
  100.1 2.0 %bitcast_convert_fusion = f32[2048,384]{1,0:T(8,128)} fusion(bf16[2,2,4,128,384]{4,3,2,1,0:T(8,128)(2,1)S(1)} %shard_map.105), kind=kLoop, calls=%fused_computation.2 | loop fusion | flops 786432 | bytes 4718592 | tf_op jit(solution)/shard_map/convert_element_type | solution.py:485
  102.2 0.0 all-gather.2.cloned.1.call-done.wq_ref.wk_ref.wv_ref.wo_ref
  102.2 0.0 copy-done.5
  102.2 0.0 copy-start.2
  102.2 2.3 %copy-done.2 = bf16[768,3072]{1,0:T(8,128)(2,1)S(1)} copy-done((bf16[768,3072]{1,0:T(8,128)(2,1)S(1)}, bf16[768,3072]{1,0:T(8,128)(2,1)}, u32[]{:S(2)}) %copy-start.2) | copy-done | bytes 4718616
  104.5 10.4 %shard_map.104 = (bf16[256,768]{1,0:T(8,128)(2,1)}, bf16[256,768]{1,0:T(8,128)(2,1)}) custom-call(s32[2]{0:T(128)S(1)} %pad_add_fusion.meta_ref, bf16[2,512,384]{2,1,0:T(8,128)(2,1)S(1)} %copy-done.5, f32[1,768]{1,0:T(1,128)S(1)} %reshape.75.gain_ref, bf16[768,3072]{1,0:T(8,128)(2,1)S(1)} %copy-done.2, bf16[768,3072]{1,0:T(8,128)(2,1)S(1)} %copy-done.2, ...), custom_call_target="tpu_custom_call" | custom-call | flops 20000000000 | bytes 20000000 | tf_op jit(solution)/shard_map/pallas_call | solution.py:407
  (2 shorter events, 0.0 us)
Async XLA Ops:
  7.2 5.3 %copy-start = (bf16[512,2048]{1,0:T(8,128)(2,1)S(1)}, bf16[512,2048]{1,0:T(8,128)(2,1)}, u32[]{:S(2)}) copy-start(bf16[512,2048]{1,0:T(8,128)(2,1)} %param.8) | copy-start | bytes 6291460
  7.2 95.0 %all-gather.2.cloned.1.call-start = ((), (), s32[]{:S(2)}) async-start(), calls=%async_computation | async-start | bytes 5013504 | tf_op jit(solution)/shard_map/all_gather | solution.py:442
  15.1 34.4 %copy-start.6 = (f32[768]{0:T(1024)S(1)}, f32[768]{0:T(1024)}, u32[]{:S(2)}) copy-start(f32[768]{0:T(1024)} %param.13) | copy-start | bytes 9220
  47.8 0.9 copy-start.3
  52.3 3.1 %copy-start.4 = (bf16[2,16,32,384]{3,2,1,0:T(8,128)(2,1)S(1)}, bf16[2,16,32,384]{3,2,1,0:T(8,128)(2,1)}, u32[]{:S(2)}) copy-start(bf16[2,16,32,384]{3,2,1,0:T(8,128)(2,1)} %copy-done.3) | copy-start | bytes 2359300
  55.3 1.6 %copy-start.1 = (bf16[2048,384]{1,0:T(8,128)(2,1)S(1)}, bf16[2048,384]{1,0:T(8,128)(2,1)}, u32[]{:S(2)}) copy-start(bf16[2048,384]{1,0:T(8,128)(2,1)} %copy.18) | copy-start | bytes 4718596
  100.1 2.0 %copy-start.5 = (bf16[2,512,384]{2,1,0:T(8,128)(2,1)S(1)}, bf16[2,512,384]{2,1,0:T(8,128)(2,1)}, u32[]{:S(2)}) copy-start(bf16[2,512,384]{2,1,0:T(8,128)(2,1)} %fusion.1.rows_ref) | copy-start | bytes 2359300
  102.2 2.3 %copy-start.2 = (bf16[768,3072]{1,0:T(8,128)(2,1)S(1)}, bf16[768,3072]{1,0:T(8,128)(2,1)}, u32[]{:S(2)}) copy-start(bf16[768,3072]{1,0:T(8,128)(2,1)} %all-gather.2.cloned.1.call-done.wq_ref.wk_ref.wv_ref.wo_ref) | copy-start | bytes 14155780
Sparse Core Ops, SparseCore 0:
  10.9 77.6 all-gather.1

commit v4 on v3

--- a/solution.py
+++ b/solution.py
@@ -148,7 +148,7 @@
             forward(k, t).wait()
 
 
-def reduce_kernel(n, src, out, pair, cross, stage_b, stage_c, arrive, *sems):
+def reduce_kernel(n, feats, slots, out, src, pair, cross, stage_b, stage_c, arrive, *sems):
     s1, r1, s2, r2, s3, r3, s4, r4, s5, r5, s6, r6 = sems
     dp, seq = lax.axis_index("dp"), lax.axis_index("seq")
     q = n // 4
@@ -171,6 +171,19 @@
     @pl.loop(1, q)
     def _(t):
         pl.semaphore_signal(barrier, device_id=along(t), device_id_type=MESH)
+
+    rows = src.shape[3]
+    tile = 512
+    for first in range(0, n * rows, tile):
+        product = lax.dot_general(
+            feats[:, first : first + tile],
+            slots[...],
+            (((0,), (0,)), ((), ())),
+            preferred_element_type=F32,
+        ).astype(BF16)
+        for i in range(tile // rows):
+            k = first // rows + i
+            src[k // (2 * q), k // q % 2, k % q] = product[i * rows : (i + 1) * rows]
 
     pl.semaphore_wait(barrier, q + 1)
 
@@ -422,7 +435,7 @@
             pltpu.VMEM((slide_len, D), BF16),
             pltpu.VMEM((steps, nearby, width), BF16),
         ],
-        compiler_params=pltpu.CompilerParams(vmem_limit_bytes=48 * 1024 * 1024),
+        compiler_params=pltpu.CompilerParams(vmem_limit_bytes=60 * 1024 * 1024),
         cost_estimate=pl.CostEstimate(
             flops=20_000_000_000, bytes_accessed=20_000_000, transcendentals=1_000_000
         ),
@@ -462,25 +475,20 @@
     )
     positions = positions.reshape(slot_rows)
     spot = jnp.arange(slide_len, dtype=jnp.int32)
-    grad_part = lax.dot_general(
-        tile_feats,
-        slot_grad.reshape(slot_rows, width),
-        (((0,), (0,)), ((), ())),
-        preferred_element_type=F32,
-    ).astype(BF16)
-    features = grad_part.shape[0]
+    features = tile_feats.shape[1]
     quarter = n // 4
     shape = (2, 2, quarter, features // n, width)
     (summed,) = exchange(
         functools.partial(reduce_kernel, n),
         3,
         [(shape, BF16)],
-        [pltpu.VMEM(shape[1:], BF16)]
+        [pltpu.VMEM(shape, BF16), pltpu.VMEM(shape[1:], BF16)]
         + [pltpu.VMEM(shape[2:], BF16)] * 4
         + [DMA((2, quarter))] * 2
         + [DMA((quarter,))] * 8
         + [DMA((2, quarter))] * 2,
-        grad_part.reshape(shape),
+        tile_feats,
+        slot_grad.reshape(slot_rows, width),
     )
     proj_grad = summed.reshape(features, width).astype(F32)
 

time: 124 us -> 119 us (0.960); the launches traced: 122 us -> 118 us
  local copies, waits for them, and re-layouts: 8.32 us -> 2.67 us
  Pallas kernels: 86.3 us -> 90 us
  matrix products: 6.33 us -> 4.35 us
    unnamed x16 -> x8, local copies, waits for them, and re-layouts: 4.93 us -> 1.7 us
    convert_element_type x1 -> x0, local copies, waits for them, and re-layouts: 3.01 us -> none  [local(): grad_part = lax.dot_general(tile_feats, slot_grad.reshape(slot_rows, widt...]
    pallas_call x2, Pallas kernels: 75.9 us -> 78.4 us  [exchange(): pl.pallas_call(kernel, out_shape=tuple((jax.ShapeDtypeStruct(shape, kind)...]
    dot_general x1 -> x0, matrix products: 2.16 us -> none  [local(): lax.dot_general(tile_feats, slot_grad.reshape(slot_rows, width), (((0,),...]
  transfers between devices with their start and end apart: 1 -> 1, of which waited for: 0 -> 0; matrix products, arithmetic and copies ran while one was open for 13% -> 10% of each run, Pallas kernels for 62% -> 66%
where the time goes in v4:
time: 119 us; the launch traced here: 118 us
  Pallas kernels  90 us (76%)
  between operations  14.9 us (13%)
  other arithmetic  6.53 us (5%)
  matrix products  4.35 us (4%)
  local copies, waits for them, and re-layouts  2.67 us (2%)
    pallas_call x2, Pallas kernels, exchange(): pl.pallas_call(kernel, out_shape=tuple((jax.ShapeDtypeStruct(shape, kind)...  78.4 us
    pallas_call x1, Pallas kernels, attend(): pl.pallas_call(functools.partial(attention_kernel, seq_count, nearby), ou...  11.6 us
    dot_general x1, matrix products, local(): jnp.dot(tile_feats, w_proj, preferred_element_type=F32).astype(BF16)  2.84 us
  transfers between devices with their start and end apart: 1, of which 0 were waited for; matrix products, arithmetic and copies ran while one was open for 10% of the time, Pallas kernels for 66%

profile of v4, /device:TPU:0, one launch (start us, length us, event | category | flops | bytes accessed | tf_op | source)
XLA Modules:
  0.0 118.5 jit_solution(18147766462240013665)
XLA Ops:
  7.2 0.0 copy-start
  7.2 0.0 all-gather.2.cloned.1.call-start
  7.2 1.8 %pad_maximum_fusion = bf16[48,3072]{1,0:T(8,128)(2,1)} fusion(bf16[48,768]{1,0:T(8,128)(2,1)} %param.15, bf16[48,2304]{1,0:T(8,128)(2,1)} %param.14), kind=kLoop, calls=%fused_computation.8 | loop fusion | flops 589824 | bytes 589824 | tf_op jit(solution)/shard_map/concatenate | solution.py:456
  9.0 0.0 all-gather.2.cloned.1.call-update
  9.1 0.5 broadcast.83
  9.6 1.3 %reduce.6 = s32[512]{0:T(512)S(1)} reduce(s32[1,512]{1,0:T(1,128)} %param.9, s32[]{:T(128)} %broadcast.83), dimensions={0}, to_apply=%param.9.reduce_sub_computation.3 | reduce | bytes 4100 | tf_op args[1]
  10.9 0.1 reshape.68.pos
  11.0 1.2 copy.13
  12.2 0.2 copy.14
  12.4 0.0 copy-done
  12.4 2.8 %convolution_convert_fusion.1 = bf16[512,384]{1,0:T(8,128)(2,1)S(1)} fusion(bf16[512,2048]{1,0:T(8,128)(2,1)} %feats.1, bf16[2048,384]{1,0:T(8,128)(2,1)S(1)} %copy-done), kind=kOutput, calls=%fused_computation.3 | convolution fusion | flops 805502976 | bytes 4063232 | tf_op jit(solution)/shard_map/dot_general | solution.py:458
  15.3 0.0 copy-start.2
  15.3 32.7 %shard_map.103 = (s32[16,1,32]{2,1,0:T(1,128)S(1)}, bf16[2,16,32,384]{3,2,1,0:T(8,128)(2,1)S(1)}, bf16[16,32,384]{2,1,0:T(8,128)(2,1)S(1)}) custom-call(s32[16,1,32]{2,1,0:T(1,128)S(1)} %reshape.68.pos, bf16[2,256,384]{2,1,0:T(8,128)(2,1)S(1)} %bitcast.19, bf16[16,32,384]{2,1,0:T(8,128)(2,1)S(1)} %bitcast.22), custom_call_target="tpu_custom_call" | custom-call | flops 10000000000 | bytes 10000000 | tf_op jit(solution)/shard_map/pallas_call | solution.py:289
  48.0 0.7 reduce.7
  48.7 0.1 eq.19
  48.8 0.0 copy-done.2
  48.8 0.6 reshape.72.gain_ref
  49.4 0.0 copy-start.1
  50.2 0.7 pad_add_fusion.meta_ref
  50.8 1.5 %fusion.rows_ref = bf16[2,512,384]{2,1,0:T(8,128)(2,1)} fusion(bf16[2,512,384]{2,1,0:T(8,128)(2,1)S(1)} %bitcast.20, s32[512]{0:T(512)S(1)} %eq.19, s32[512]{0:T(512)S(1)} %fusion.11), kind=kOutput, calls=%fused_computation.2 | convolution fusion | flops 403308544 | bytes 1576960 | tf_op jit(solution)/shard_map/ps,csw->cpw/dot_general | solution.py:498
  52.3 0.0 copy-done.1
  52.4 45.6 %shard_map.105 = bf16[2,2,4,128,384]{4,3,2,1,0:T(8,128)(2,1)S(1)} custom-call(bf16[512,2048]{1,0:T(8,128)(2,1)S(1)} %copy-done.1, bf16[512,384]{1,0:T(8,128)(2,1)S(1)} %bitcast.21), custom_call_target="tpu_custom_call" | custom-call | flops 10000000000 | bytes 10000000 | tf_op jit(solution)/shard_map/pallas_call | solution.py:289
  98.0 2.0 %bitcast_convert_fusion = f32[2048,384]{1,0:T(8,128)} fusion(bf16[2,2,4,128,384]{4,3,2,1,0:T(8,128)(2,1)S(1)} %shard_map.105), kind=kLoop, calls=%fused_computation | loop fusion | flops 786432 | bytes 4718592 | tf_op jit(solution)/shard_map/convert_element_type | solution.py:493
  100.0 0.0 all-gather.2.cloned.1.call-done.wq_ref.wk_ref.wv_ref.wo_ref
  100.0 11.6 %shard_map.104 = (bf16[256,768]{1,0:T(8,128)(2,1)}, bf16[256,768]{1,0:T(8,128)(2,1)}) custom-call(s32[2]{0:T(128)} %pad_add_fusion.meta_ref, bf16[2,512,384]{2,1,0:T(8,128)(2,1)} %fusion.rows_ref, f32[1,768]{1,0:T(1,128)} %reshape.72.gain_ref, bf16[768,3072]{1,0:T(8,128)(2,1)} %all-gather.2.cloned.1.call-done.wq_ref.wk_ref.wv_ref.wo_ref, ...), custom_call_target="tpu_custom_call" | custom-call | flops 20000000000 | bytes 20000000 | tf_op jit(solution)/shard_map/pallas_call | solution.py:420
  (1 shorter events, 0.0 us)
Async XLA Ops:
  7.2 5.2 %copy-start = (bf16[2048,384]{1,0:T(8,128)(2,1)S(1)}, bf16[2048,384]{1,0:T(8,128)(2,1)}, u32[]{:S(2)}) copy-start(bf16[2048,384]{1,0:T(8,128)(2,1)} %param.11) | copy-start | bytes 4718596
  7.2 92.8 %all-gather.2.cloned.1.call-start = ((), (), s32[]{:S(2)}) async-start(), calls=%async_computation | async-start | bytes 5013504 | tf_op jit(solution)/shard_map/all_gather | solution.py:455
  15.3 33.5 %copy-start.2 = (f32[768]{0:T(1024)S(1)}, f32[768]{0:T(1024)}, u32[]{:S(2)}) copy-start(f32[768]{0:T(1024)} %param.13) | copy-start | bytes 9220
  49.4 3.0 %copy-start.1 = (bf16[512,2048]{1,0:T(8,128)(2,1)S(1)}, bf16[512,2048]{1,0:T(8,128)(2,1)}, u32[]{:S(2)}) copy-start(bf16[512,2048]{1,0:T(8,128)(2,1)} %feats.1) | copy-start | bytes 6291460
Sparse Core Ops, SparseCore 0:
  10.9 84.4 all-gather.1
